TPU v7x, 256 devices: a whole 4x4x8 slice. The times are simulated.
256 devices in a mesh: sub: 64 (over y, z, core), grp: 4 (over x).
Axes of the slice: x: 4, y: 4, z: 8, core: 2. Of those that a mesh axis runs over, the one named last changes fastest.
Arguments:
- schur: bfloat16 [512, 1536, 1536], P(('sub', 'grp')), as said below
- local_gap: float32 [512, 1536, 128], P(('sub', 'grp')), may hold values from -6 to 6
- modes: float32 [512, 6, 1536], P(('sub', 'grp')), may hold values from -0.45927933 to 0.45927933
- rigid_loads: float32 [512, 6, 128], P(('sub', 'grp')), may hold values from -6 to 6
- coarse_inverse: float32 [3072, 3072], P(('sub', 'grp')), as said below
- block_slot: int32 [512, 12], P(('sub', 'grp')), may hold values from 0 to 11, each once within a row
- face_swap: int32 [512, 6], P(('sub', 'grp')), may hold values from 0 to 1, as said below
- lengths: int32 [512, 12], P(('sub', 'grp')), may hold values from 0 to 128, as said below
Outputs:
- multipliers: float32 [512, 1536, 128], P(('sub', 'grp'))
- residual_ratio: float32 [128], replicated
Inputs may be any that keep to these rules, and one draw needn't show every extreme that they name: `schur`: each schur_s is symmetric positive definite. coarse_inverse is symmetric with a positive diagonal and small off-diagonal entries. `face_swap`: two subdomains that share a face hold the same value for it; absent faces hold any value. A slot and its partner slot have equal lengths; slots of absent faces have length 0; on every face toward a neighbour along sub one copy has length 128.
All inputs are finite; a program needn't handle non-finite values.
Results may differ from a plain program's by a relative error of at most 0.00075.
Values sent between devices are 32-bit elements; how exact they have to be, the bound alone decides.
No kernel may reach another device: no remote copies, remote signals or barrier semaphores. Data moves between devices by JAX's collectives and lax.ppermute only.
A program may use at most 128 MiB of HBM per device.

v0:
```python
import jax
import jax.numpy as jnp
from jax import lax
from jax.sharding import PartitionSpec as P

ITERS = 2


HIGH = lax.Precision.HIGHEST


def passed_along(block, axis, distance):
    devices = range(lax.axis_size(axis))
    route = [(i - distance, i) for i in devices if i - distance in devices]
    return lax.ppermute(block, axis, route)


def from_behind(value, axis, steps):
    count = lax.axis_size(axis)
    pairs = [(source, (source + steps) % count) for source in range(count)]
    return lax.ppermute(value, axis, pairs)


def build_layout(block_slot, face_swap, lengths, width):
    blocks = block_slot.shape[1]
    tile = width // blocks
    order = jnp.arange(blocks, dtype=jnp.int32)
    hits = block_slot[:, None, :] == order[None, :, None]
    slot_pos = jnp.sum(jnp.where(hits, order[None, None, :], 0), axis=2)
    face = block_slot // 2
    copy_index = block_slot % 2
    swapped = jnp.take_along_axis(face_swap, face, axis=1)
    take_index = face * 2 + (copy_index + swapped) % 2
    live = jnp.take_along_axis(lengths, block_slot, axis=1)
    rows = jnp.arange(tile, dtype=jnp.int32)
    mask = (rows[None, None, :, None] < live[:, :, None, None]).astype(jnp.float32)
    return (slot_pos, take_index, mask)


def send_fields(by_slot):
    group_lower = passed_along(by_slot[:, 6:8], "grp", 1)
    group_upper = passed_along(by_slot[:, 4:6], "grp", -1)
    cycle_lower = from_behind(by_slot[:, 10:12], "sub", 1)
    cycle_upper = from_behind(by_slot[:, 8:10], "sub", -1)
    return [group_lower, group_upper, cycle_lower, cycle_upper]


def face_partners(values, layout, sender):
    slot_pos, take_index, mask = layout
    count, width, cases = values.shape
    blocks = slot_pos.shape[1]
    tiles = values.reshape(count, blocks, width // blocks, cases)
    by_slot = jnp.take_along_axis(tiles, slot_pos[:, :, None, None], axis=1)
    empty = jnp.zeros_like(by_slot[:1, 0:2])
    from_lower = jnp.concatenate([empty, by_slot[:-1, 2:4]], axis=0)
    from_upper = jnp.concatenate([by_slot[1:, 0:2], empty], axis=0)
    incoming = jnp.concatenate([from_lower, from_upper] + sender(by_slot), axis=1)
    picked = jnp.take_along_axis(incoming, take_index[:, :, None, None], axis=1)
    return (tiles, picked)


def exchange_faces(values, layout):
    tiles, picked = face_partners(values, layout, send_fields)
    return ((tiles - picked) * layout[2]).reshape(values.shape)


def apply_local(schur, vector):
    return jnp.einsum(
        "kij,kjr->kir", schur, vector.astype(jnp.bfloat16), preferred_element_type=jnp.float32
    )


def mode_terms(modes, vector):
    return jnp.einsum("kmn,knr->kmr", modes, vector, precision=HIGH)


def lift(modes, coarse):
    return jnp.einsum("kmn,kmr->knr", modes, coarse, precision=HIGH)


def dual_dot(left, right):
    return jnp.sum(left * right, axis=(0, 1))


def global_norm(vector):
    return lax.psum(dual_dot(vector, vector), ("sub", "grp"))


def body(schur, local_gap, modes, rigid_loads, coarse_inverse, block_slot, face_swap, lengths):
    count, width, cases = local_gap.shape
    mode_count = modes.shape[1]
    layout = build_layout(block_slot, face_swap, lengths, width)

    def lifted(coarse):
        return exchange_faces(lift(modes, coarse), layout)

    def coarse_apply(terms):
        piece = lax.all_gather(terms, ("sub", "grp"), axis=0, tiled=True)
        span = piece.shape[0] * piece.shape[1]
        solved = jnp.dot(coarse_inverse, piece.reshape(span, cases), precision=HIGH)
        return solved.reshape(count, mode_count, cases)

    multipliers = lifted(coarse_apply(rigid_loads))
    residual = exchange_faces(local_gap - apply_local(schur, multipliers), layout)
    residual_coarse = coarse_apply(mode_terms(modes, residual))
    projected = residual - lifted(residual_coarse)
    norm_now = global_norm(projected)
    first = norm_now
    direction = projected
    for step in range(ITERS):
        image = exchange_faces(apply_local(schur, direction), layout)
        curvature = lax.psum(dual_dot(direction, image), ("sub", "grp"))
        alpha = norm_now / curvature
        multipliers = multipliers + alpha * direction
        residual = residual - alpha * image
        residual_coarse = coarse_apply(mode_terms(modes, residual))
        projected = residual - lifted(residual_coarse)
        fresh = global_norm(projected)
        if step + 1 < ITERS:
            direction = projected + fresh / norm_now * direction
        norm_now = fresh
    return (multipliers, jnp.sqrt(norm_now / first))


def solution(mesh):
    in_specs = (
        P(("sub", "grp"), None, None),
        P(("sub", "grp"), None, None),
        P(("sub", "grp"), None, None),
        P(("sub", "grp"), None, None),
        P(("sub", "grp"), None),
        P(("sub", "grp"), None),
        P(("sub", "grp"), None),
        P(("sub", "grp"), None),
    )
    out_specs = (P(("sub", "grp"), None, None), P())
    return jax.shard_map(body, mesh=mesh, in_specs=in_specs, out_specs=out_specs, check_vma=False)
```

profile of v0, /device:TPU:1, one launch (start us, length us, event | category | flops | bytes accessed | tf_op | source)
XLA Modules:
  0.0 994.7 jit_solution(11286170232813215243)
XLA Ops:
  14.7 105.3 %all-gather.5.cloned.1.call-done = f32[512,6,128]{2,1,0:T(8,128)} async-done(((f32[2,6,128]{2,1,0:T(8,128)}), f32[512,6,128]{2,1,0:T(8,128)}) %all-gather.5.cloned.1.call-update) | async-done | bytes 1572880 | tf_op jit(solution)/shard_map/all_gather | solution.py:98
  123.6 2.6 convolution_bitcast_fusion.6
  131.7 2.9 collective-permute-start
  140.8 2.8 collective-permute-done.1
  145.7 3.3 gather_fusion.3
  152.2 6.9 fusion
  160.6 3.1 collective-permute-start.4
  163.7 4.8 collective-permute-start.7
  170.4 5.3 collective-permute-done.5
  181.2 104.5 %all-gather.7.cloned.1.call-done = f32[512,6,128]{2,1,0:T(8,128)} async-done(((f32[2,6,128]{2,1,0:T(8,128)}), f32[512,6,128]{2,1,0:T(8,128)}) %all-gather.7.cloned.1.call-update) | async-done | bytes 1572880 | tf_op jit(solution)/shard_map/all_gather | solution.py:98
  288.3 2.6 convolution_bitcast_fusion.4
  296.4 2.9 collective-permute-start.8
  305.5 2.8 collective-permute-done.9
  310.5 3.3 gather_fusion.7
  318.2 8.2 convolution_bitcast_fusion.3
  331.9 3.1 collective-permute-start.12
  335.0 4.8 collective-permute-start.15
  341.4 5.7 collective-permute-done.13
  349.2 3.5 multiply_reduce_fusion.2
  352.7 79.0 %all-reduce.14 = (f32[128]{0:T(128)S(1)}, f32[128]{0:T(128)S(1)}) all-reduce(f32[128]{0:T(128)S(1)} %get-tuple-element.4, f32[128]{0:T(128)S(1)} %get-tuple-element.3), channel_id=1, replica_groups=mesh['sub'=64,'grp'=4] {'sub','grp'}, use_global_device_ids=true, to_apply=%region_2.4 | all-reduce | flops 256 | bytes 2048 | tf_op jit(solution)/shard_map/psum | solution.py:86
  434.6 99.4 %all-gather.9.cloned.1.call-done = f32[512,6,128]{2,1,0:T(8,128)} async-done(((f32[2,6,128]{2,1,0:T(8,128)}), f32[512,6,128]{2,1,0:T(8,128)}) %all-gather.9.cloned.1.call-update) | async-done | bytes 1572880 | tf_op jit(solution)/shard_map/all_gather | solution.py:98
  534.0 2.7 reshape.133
  539.1 2.6 convolution_bitcast_fusion.2
  541.7 3.1 copy.79
  544.8 3.3 gather_fusion.10
  549.7 2.9 collective-permute-start.16
  558.9 2.8 collective-permute-done.17
  563.8 3.2 gather_fusion.11
  567.1 3.4 multiply_reduce_fusion.1
  570.5 79.0 %psum.37 = f32[128]{0:T(128)S(1)} all-reduce(f32[128]{0:T(128)S(1)} %get-tuple-element.9), channel_id=1, replica_groups=mesh['sub'=64,'grp'=4] {'sub','grp'}, use_global_device_ids=true, to_apply=%region_6.8 | all-reduce | flops 128 | bytes 1024 | tf_op jit(solution)/shard_map/psum | solution.py:86
  649.5 2.6 fusion.2
  653.3 8.2 convolution_bitcast_fusion.1
  661.6 3.0 copy.81
  664.6 3.3 gather_fusion.12
  677.5 6.2 collective-permute-done.21
  685.8 3.3 gather_fusion.13
  689.1 4.1 multiply_reduce_fusion
  693.2 73.4 %psum.38 = f32[128]{0:T(128)S(1)} all-reduce(f32[128]{0:T(128)S(1)} %get-tuple-element.7), channel_id=1, replica_groups=mesh['sub'=64,'grp'=4] {'sub','grp'}, use_global_device_ids=true, to_apply=%region_8.10 | all-reduce | flops 128 | bytes 1024 | tf_op jit(solution)/shard_map/psum | solution.py:112
  766.7 4.8 fusion.1
  773.1 99.7 %all-gather.11.cloned.1.call-done = f32[512,6,128]{2,1,0:T(8,128)} async-done(((f32[2,6,128]{2,1,0:T(8,128)}), f32[512,6,128]{2,1,0:T(8,128)}) %all-gather.11.cloned.1.call-update) | async-done | bytes 1572880 | tf_op jit(solution)/shard_map/all_gather | solution.py:98
  877.7 2.6 convolution_bitcast_fusion
  880.3 3.1 copy.84
  883.3 3.3 gather_fusion.14
  888.3 2.9 collective-permute-start.24
  897.4 2.8 collective-permute-done.25
  902.4 3.2 gather_fusion.15
  905.6 2.7 fusion.8
  908.3 79.1 %psum.39 = f32[128]{0:T(128)S(1)} all-reduce(f32[128]{0:T(128)S(1)} %fusion.8), channel_id=1, replica_groups=mesh['sub'=64,'grp'=4] {'sub','grp'}, use_global_device_ids=true, to_apply=%region_10.12 | all-reduce | flops 128 | bytes 1024 | tf_op jit(solution)/shard_map/psum | solution.py:86
  (187 shorter events, 111.7 us)
Async XLA Ops:
  7.2 116.4 %copy-start = (f32[2,6,1536]{2,0,1:T(2,128)S(1)}, f32[2,6,1536]{2,0,1:T(2,128)}, u32[]{:S(2)}) copy-start(f32[2,6,1536]{2,0,1:T(2,128)} %param.12) | copy-start | bytes 221188
  7.2 5.8 copy-start.10
  7.2 4.8 copy-start.1
  7.2 6.2 copy-start.8
  7.2 6.9 copy-start.9
  7.2 112.8 %all-gather.5.cloned.1.call-start = ((), (), s32[]{:S(2)}) async-start(), calls=%async_computation | async-start | bytes 2105344 | tf_op jit(solution)/shard_map/all_gather | solution.py:98
  8.7 277.0 %all-gather.7.cloned.1.call-start = ((), (), s32[]{:S(2)}) async-start(), calls=%async_computation.1 | async-start | bytes 2105344 | tf_op jit(solution)/shard_map/all_gather | solution.py:98
  131.7 8.4 collective-permute-start
  134.6 10.4 %collective-permute-start.3 = (f32[2,2,128,128]{3,2,1,0:T(8,128)S(1)}, f32[2,2,128,128]{3,2,1,0:T(8,128)S(1)}, u32[]{:S(2)}, u32[]{:S(2)}) collective-permute-start(f32[2,2,128,128]{3,2,1,0:T(8,128)S(1)} %get-tuple-element.52), channel_id=1, source_target_pairs={{0,252},{4,0},{8,4},{12,8},{16,12},{20,16},{24,20},{28,24},{32,28}... | collective-permute-start | bytes 786440 | tf_op jit(solution)/shard_map/ppermute | solution.py:21
  135.2 9.1 collective-permute-start.2
  136.5 7.1 collective-permute-start.1
  150.9 1.2 copy-start.6
  160.6 9.7 collective-permute-start.4
  163.7 12.0 %collective-permute-start.7 = (f32[2,2,128,128]{3,2,1,0:T(8,128)S(1)}, f32[2,2,128,128]{3,2,1,0:T(8,128)S(1)}, u32[]{:S(2)}, u32[]{:S(2)}) collective-permute-start(f32[2,2,128,128]{3,2,1,0:T(8,128)S(1)} %get-tuple-element.46), channel_id=1, source_target_pairs={{0,252},{4,0},{8,4},{12,8},{16,12},{20,16},{24,20},{28,24},{32,28}... | collective-permute-start | bytes 786440 | tf_op jit(solution)/shard_map/ppermute | solution.py:21
  168.5 7.1 collective-permute-start.6
  168.5 7.1 collective-permute-start.5
  181.1 352.9 %all-gather.9.cloned.1.call-start = ((), (), s32[]{:S(2)}) async-start(), calls=%async_computation.2 | async-start | bytes 2105344 | tf_op jit(solution)/shard_map/all_gather | solution.py:98
  296.4 8.4 collective-permute-start.8
  299.4 10.4 %collective-permute-start.11 = (f32[2,2,128,128]{3,2,1,0:T(8,128)S(1)}, f32[2,2,128,128]{3,2,1,0:T(8,128)S(1)}, u32[]{:S(2)}, u32[]{:S(2)}) collective-permute-start(f32[2,2,128,128]{3,2,1,0:T(8,128)S(1)} %get-tuple-element.40), channel_id=1, source_target_pairs={{0,252},{4,0},{8,4},{12,8},{16,12},{20,16},{24,20},{28,24},{32,28}... | collective-permute-start | bytes 786440 | tf_op jit(solution)/shard_map/ppermute | solution.py:21
  300.0 9.1 collective-permute-start.10
  301.2 7.1 collective-permute-start.9
  315.7 1.1 copy-start.4
  317.0 1.2 copy-start.2
  328.2 2.0 copy-start.5
  331.9 9.5 collective-permute-start.12
  335.0 12.2 %collective-permute-start.15 = (f32[2,2,128,128]{3,2,1,0:T(8,128)S(1)}, f32[2,2,128,128]{3,2,1,0:T(8,128)S(1)}, u32[]{:S(2)}, u32[]{:S(2)}) collective-permute-start(f32[2,2,128,128]{3,2,1,0:T(8,128)S(1)} %get-tuple-element.34), channel_id=1, source_target_pairs={{0,252},{4,0},{8,4},{12,8},{16,12},{20,16},{24,20},{28,24},{32,28}... | collective-permute-start | bytes 786440 | tf_op jit(solution)/shard_map/ppermute | solution.py:21
  339.8 7.3 collective-permute-start.14
  340.0 7.1 collective-permute-start.13
  431.9 1.1 copy-start.3
  434.6 438.2 %all-gather.11.cloned.1.call-start = ((), (), s32[]{:S(2)}) async-start(), calls=%async_computation.3 | async-start | bytes 2105344 | tf_op jit(solution)/shard_map/all_gather | solution.py:98
  549.7 8.4 collective-permute-start.16
  552.7 10.4 %collective-permute-start.19 = (f32[2,2,128,128]{3,2,1,0:T(8,128)S(1)}, f32[2,2,128,128]{3,2,1,0:T(8,128)S(1)}, u32[]{:S(2)}, u32[]{:S(2)}) collective-permute-start(f32[2,2,128,128]{3,2,1,0:T(8,128)S(1)} %get-tuple-element.28), channel_id=1, source_target_pairs={{0,252},{4,0},{8,4},{12,8},{16,12},{20,16},{24,20},{28,24},{32,28}... | collective-permute-start | bytes 786440 | tf_op jit(solution)/shard_map/ppermute | solution.py:21
  553.3 9.1 collective-permute-start.18
  554.5 7.1 collective-permute-start.17
  652.1 1.2 copy-start.7
  669.6 7.1 collective-permute-start.20
  671.8 13.3 %collective-permute-start.23 = (f32[2,2,128,128]{3,2,1,0:T(8,128)S(1)}, f32[2,2,128,128]{3,2,1,0:T(8,128)S(1)}, u32[]{:S(2)}, u32[]{:S(2)}) collective-permute-start(f32[2,2,128,128]{3,2,1,0:T(8,128)S(1)} %get-tuple-element.22), channel_id=1, source_target_pairs={{0,252},{4,0},{8,4},{12,8},{16,12},{20,16},{24,20},{28,24},{32,28}... | collective-permute-start | bytes 786440 | tf_op jit(solution)/shard_map/ppermute | solution.py:21
  672.9 11.5 %collective-permute-start.22 = (f32[2,2,128,128]{3,2,1,0:T(8,128)S(1)}, f32[2,2,128,128]{3,2,1,0:T(8,128)S(1)}, u32[]{:S(2)}, u32[]{:S(2)}) collective-permute-start(f32[2,2,128,128]{3,2,1,0:T(8,128)S(1)} %get-tuple-element.23), channel_id=1, source_target_pairs={{0,4},{4,8},{8,12},{12,16},{16,20},{20,24},{24,28},{28,32},{32,36}... | collective-permute-start | bytes 786440 | tf_op jit(solution)/shard_map/ppermute | solution.py:21
  673.6 10.0 %collective-permute-start.21 = (f32[2,2,128,128]{3,2,1,0:T(8,128)S(1)}, f32[2,2,128,128]{3,2,1,0:T(8,128)S(1)}, u32[]{:S(2)}, u32[]{:S(2)}) collective-permute-start(f32[2,2,128,128]{3,2,1,0:T(8,128)S(1)} %get-tuple-element.24), channel_id=1, source_target_pairs={{1,0},{2,1},{3,2},{5,4},{6,5},{7,6},{9,8},{10,9},{11,10},{13,12},{... | collective-permute-start | bytes 786440 | tf_op jit(solution)/shard_map/ppermute | solution.py:15
  888.3 8.4 collective-permute-start.24
  891.3 10.4 %collective-permute-start.27 = (f32[2,2,128,128]{3,2,1,0:T(8,128)S(1)}, f32[2,2,128,128]{3,2,1,0:T(8,128)S(1)}, u32[]{:S(2)}, u32[]{:S(2)}) collective-permute-start(f32[2,2,128,128]{3,2,1,0:T(8,128)S(1)} %get-tuple-element.16), channel_id=1, source_target_pairs={{0,252},{4,0},{8,4},{12,8},{16,12},{20,16},{24,20},{28,24},{32,28}... | collective-permute-start | bytes 786440 | tf_op jit(solution)/shard_map/ppermute | solution.py:21
  891.8 9.1 collective-permute-start.26
  893.1 7.1 collective-permute-start.25
Sparse Core Ops, SparseCore 0:
  11.8 108.1 all-gather.4
  181.3 104.4 all-gather.6
  434.7 99.2 all-gather.8
  773.2 99.5 all-gather.10
where the time goes:
time: 1000 us; the launch traced here: 995 us
  waiting for transfers between devices  441 us (44%)
  blocking collectives  311 us (31%)
  local copies, waits for them, and re-layouts  94.4 us (9%)
  starting transfers between devices  48.7 us (5%)
  matrix products  46 us (5%)
  other arithmetic  39.2 us (4%)
  between operations  14.7 us (1%)
    all_gather x4, waiting for transfers between devices, coarse_apply(): piece = lax.all_gather(terms, ('sub', 'grp'), axis=0, tiled=True)  409 us
    psum x3, blocking collectives, global_norm(): return lax.psum(dual_dot(vector, vector), ('sub', 'grp'))  237 us
    psum x1, blocking collectives, body(): curvature = lax.psum(dual_dot(direction, image), ('sub', 'grp'))  73.4 us
    ppermute x14, waiting for transfers between devices, passed_along(): return lax.ppermute(block, axis, route)  32.1 us
    ppermute x14, starting transfers between devices, passed_along(): return lax.ppermute(block, axis, route)  29.5 us
    unnamed x59, local copies, waits for them, and re-layouts  25.9 us
    dot_general x3, matrix products, apply_local(): jnp.einsum('kij,kjr->kir', schur, vector.astype(jnp.bfloat16), preferred_...  23.3 us
    gather x8, local copies, waits for them, and re-layouts, face_partners(): picked = jnp.take_along_axis(incoming, take_index[:, :, None, None], axis=1)  20.4 us
  transfers between devices with their start and end apart: 32, of which 16 were waited for; matrix products, arithmetic and copies ran while one was open for 2% of the time, Pallas kernels for 0%

commit v1 on v0

v1 whole, which is shorter than its diff:
```python
import functools

import jax
import jax.numpy as jnp
from jax import lax
from jax.experimental import pallas as pl
from jax.experimental.pallas import tpu as pltpu
from jax.sharding import Mesh, PartitionSpec as P

BLK = 128
SLOTS = 12
MODES = 6
ROWS = 16
SPLIT_LEFT = (0, 0, 1, 0, 1, 2)
SPLIT_RIGHT = (0, 1, 0, 2, 1, 0)
F32 = jnp.float32
BF16 = jnp.bfloat16
VMEM = pl.BlockSpec(memory_space=pltpu.VMEM)
SMEM = pl.BlockSpec(memory_space=pltpu.SMEM)
ANY = pl.BlockSpec(memory_space=pl.ANY)


def shape(*dims, kind=F32):
    return jax.ShapeDtypeStruct(dims, kind)


def call(kernel, out, in_specs, scratch=(), flops=0, moved=0):
    return pl.pallas_call(
        kernel,
        out_shape=out,
        in_specs=in_specs,
        out_specs=jax.tree.map(lambda _: VMEM, out),
        scratch_shapes=list(scratch),
        compiler_params=pltpu.CompilerParams(vmem_limit_bytes=50 * 2**20),
        cost_estimate=pl.CostEstimate(flops=flops, bytes_accessed=moved, transcendentals=0),
    )


def thirds(value):
    first = value.astype(BF16)
    rest = value - first.astype(F32)
    second = rest.astype(BF16)
    third = (rest - second.astype(F32)).astype(BF16)
    return first, second, third


def modes_kernel(slot_ref, modes_ref, split_ref, *rest):
    parts, by_slot = rest[:5], rest[5]
    by_slot[...] = jnp.zeros_like(by_slot)
    for k in range(2):
        for b in range(SLOTS):
            by_slot[k, slot_ref[k, b], 0:MODES] = modes_ref[k, :, b * BLK:(b + 1) * BLK]
    parts[0][...] = by_slot[:, 0:4]
    for n in range(4):
        parts[n + 1][...] = by_slot[:, 4 + 2 * n:6 + 2 * n]
    for k in range(2):
        for q in range(SLOTS):
            pieces = [piece.astype(F32) for piece in thirds(by_slot[k, q])]
            pieces.append(jnp.zeros_like(pieces[0]))
            split_ref[k, :, q * BLK:(q + 1) * BLK] = jnp.concatenate(pieces, axis=0).astype(BF16)


def arrange_modes(slots, modes):
    return call(
        modes_kernel,
        (shape(2, 32, SLOTS * BLK, kind=BF16), shape(2, 4, 8, BLK)) + (shape(2, 2, 8, BLK),) * 4,
        [SMEM, VMEM],
        [pltpu.VMEM((2, SLOTS, 8, BLK), F32)],
    )(slots, modes)


def partner(parts, arrived, swap_ref, k, f, c):
    meets = jnp.bitwise_xor(swap_ref[k, f], c)
    if f == 0:
        return parts[0][1 - k, 2 + meets]
    if f == 1:
        return parts[0][1 - k, meets]
    return arrived[f - 2][k, meets]


def own(parts, k, f, c):
    return parts[0][k, 2 * f + c] if f < 2 else parts[f - 1][k, c]


def partial_kernel(before_ref, here_ref, after_ref, terms_ref, out_ref):
    terms = terms_ref[...].reshape(-1, BLK)
    high = functools.partial(jnp.dot, precision=lax.Precision.HIGHEST, preferred_element_type=F32)
    before = high(before_ref[...], terms)
    here = high(here_ref[...], terms)
    after = high(after_ref[...], terms)
    tables = [before, here[0:64], here[64:128], after]
    sums = jnp.sum(terms_ref[:, 8:16, :], axis=0)
    upper = lax.broadcasted_iota(jnp.int32, (8, BLK), 0) >= 4

    def rows(table, x):
        return tables[table][x * ROWS:(x + 1) * ROWS]

    for core in range(2):
        for x in range(4):
            d = core * 4 + x
            mine = rows(1 + core, x)
            out_ref[d, 0, 0:8] = mine[0:8]
            out_ref[d, 0, 8:16] = jnp.where(upper, sums, mine[8:16])
            out_ref[d, 1] = rows(1 + core, max(x - 1, 0))
            out_ref[d, 2] = rows(1 + core, min(x + 1, 3))
            out_ref[d, 3] = rows(core, x)
            out_ref[d, 4] = rows(2 + core, x)


def coarse_solve(table, terms):
    gathered = lax.all_to_all(terms, "p", 0, 0, tiled=True)
    partial = call(partial_kernel, shape(8, 5, ROWS, BLK), [VMEM] * 4)(*table, gathered)
    return lax.all_to_all(partial, ("core", "x"), 0, 0, tiled=True)


def load_coefficients(partial_ref, coef_ref):
    solved = jnp.sum(partial_ref[...], axis=0)
    coef_ref[...] = jnp.zeros_like(coef_ref)
    for k in range(2):
        lines = slice(MODES * k, MODES * (k + 1))
        other = slice(MODES * (1 - k), MODES * (2 - k))
        for f in range(6):
            coef_ref[k, f, 0:MODES] = solved[0, lines]
            coef_ref[k, f, MODES:2 * MODES] = solved[0, other] if f < 2 else solved[f - 1, lines]
    return solved[0]


def lifted(lift_ref, coef_ref, k, f):
    pieces = thirds(coef_ref[k, f])
    right = jnp.concatenate([pieces[n] for n in SPLIT_RIGHT], axis=0)
    return jnp.dot(lift_ref[k, f], right, preferred_element_type=F32)


def fetch_schur(schur_ref, held, sems):
    copies = []
    for k in range(2):
        for n in range(3):
            rows = pl.ds(n * 512, 512)
            copy = pltpu.make_async_copy(schur_ref.at[k, rows], held.at[k, rows], sems.at[3 * k + n])
            copy.start()
            copies.append(copy)
    return copies


def apply_schur(copies, held, rounded, slot_ref, by_slot, parts, base=None):
    for k in range(2):
        for n in range(3):
            copies[3 * k + n].wait()
            image = jnp.dot(held[k, n * 512:(n + 1) * 512], rounded[k], preferred_element_type=F32)
            for j in range(4):
                b = 4 * n + j
                piece = image[j * BLK:(j + 1) * BLK]
                if base is not None:
                    piece = base[k, b * BLK:(b + 1) * BLK] - piece
                by_slot[slot_ref[k, b]] = piece
        parts[0][k] = by_slot[0:4]
        for n in range(4):
            parts[n + 1][k] = by_slot[4 + 2 * n:6 + 2 * n]


def round_blocks(field_ref, slot_ref, rounded):
    for k in range(2):
        for b in range(SLOTS):
            rounded[k, b * BLK:(b + 1) * BLK] = field_ref[k, slot_ref[k, b]].astype(BF16)


PARTS = (shape(2, 4, BLK, BLK),) + (shape(2, 2, BLK, BLK),) * 4
FIELD = shape(2, SLOTS, BLK, BLK)
SCRATCH = [
    pltpu.VMEM((2, 6, ROWS, BLK), F32),
    pltpu.VMEM((2, SLOTS * BLK, SLOTS * BLK), BF16),
    pltpu.VMEM((2, SLOTS * BLK, BLK), BF16),
    pltpu.VMEM((SLOTS, BLK, BLK), F32),
    pltpu.SemaphoreType.DMA((6,)),
]


def first_kernel(slot_ref, swap_ref, length_ref, partial_ref, gap_ref, schur_ref, *rest):
    parts, arrived = rest[0:5], rest[5:9]
    lift_ref, field_ref = rest[9:11]
    images = rest[11:16]
    coef_ref, held, rounded, by_slot, sems = rest[16:]
    copies = fetch_schur(schur_ref, held, sems)
    lane = lax.broadcasted_iota(jnp.int32, (8, BLK), 1)
    for k in range(2):
        for f in range(6):
            for c in range(2):
                live = lane < length_ref[k, 2 * f + c]
                mine = jnp.where(live, own(parts, k, f, c), 0.0)
                theirs = jnp.where(live, -partner(parts, arrived, swap_ref, k, f, c), 0.0)
                both = jnp.concatenate([mine[0:MODES], theirs[0:MODES], mine[MODES:8], mine[MODES:8]], axis=0)
                pieces = [piece.astype(F32) for piece in thirds(both)]
                left = jnp.concatenate([pieces[n] for n in SPLIT_LEFT], axis=0)
                lift_ref[k, f, c * BLK:(c + 1) * BLK] = left.T.astype(BF16)
    load_coefficients(partial_ref, coef_ref)
    for k in range(2):
        for f in range(6):
            field_ref[k, 2 * f:2 * f + 2] = lifted(lift_ref, coef_ref, k, f).reshape(2, BLK, BLK)
    round_blocks(field_ref, slot_ref, rounded)
    apply_schur(copies, held, rounded, slot_ref, by_slot, images, gap_ref)


def project_kernel(slot_ref, partial_ref, lift_ref, schur_ref, residual_ref, *rest):
    field_ref, images = rest[0], rest[1:6]
    coef_ref, held, rounded, by_slot, sems = rest[6:]
    copies = fetch_schur(schur_ref, held, sems)
    load_coefficients(partial_ref, coef_ref)
    for k in range(2):
        for f in range(6):
            lift = lifted(lift_ref, coef_ref, k, f).reshape(2, BLK, BLK)
            field_ref[k, 2 * f:2 * f + 2] = residual_ref[k, 2 * f:2 * f + 2] - lift
    round_blocks(field_ref, slot_ref, rounded)
    apply_schur(copies, held, rounded, slot_ref, by_slot, images)


def step_kernel(slot_ref, partial_ref, lift_ref, schur_ref, image_ref, projected_ref, *rest):
    sums_ref, change_ref, field_ref, images = rest[0], rest[1], rest[2], rest[3:8]
    coef_ref, held, rounded, by_slot, sems = rest[8:]
    copies = fetch_schur(schur_ref, held, sems)
    sums = load_coefficients(partial_ref, coef_ref)[8:16]
    sums_ref[...] = sums
    alpha = sums[4:5] / sums[5:6]
    for k in range(2):
        for f in range(6):
            pair = slice(2 * f, 2 * f + 2)
            change = image_ref[k, pair] - lifted(lift_ref, coef_ref, k, f).reshape(2, BLK, BLK)
            change_ref[k, pair] = change
            field_ref[k, pair] = projected_ref[k, pair] - alpha[None] * change
    round_blocks(field_ref, slot_ref, rounded)
    apply_schur(copies, held, rounded, slot_ref, by_slot, images)


def last_kernel(
    slot_ref, partial_ref, lift_ref, sums_ref, start_ref, first_ref, change_ref, second_ref, image_ref,
    multipliers_ref, norm_ref, coef_ref, by_slot,
):
    riders = load_coefficients(partial_ref, coef_ref)
    start_norm, start_curve = sums_ref[4:5], sums_ref[5:6]
    norm, second_curve, cross, back = riders[12:13], riders[13:14], riders[14:15], riders[15:16]
    alpha = start_norm / start_curve
    beta = norm / start_norm
    curve = second_curve + beta * (cross + back) + beta * beta * start_curve
    step = norm / curve
    total = jnp.zeros((1, BLK), F32)
    for k in range(2):
        for f in range(6):
            pair = slice(2 * f, 2 * f + 2)
            lift = lifted(lift_ref, coef_ref, k, f).reshape(2, BLK, BLK)
            change = (image_ref[k, pair] - lift) + beta[None] * change_ref[k, pair]
            second = second_ref[k, pair]
            left = second - step[None] * change
            total = total + jnp.sum((left * left).reshape(2 * BLK, BLK), axis=0, keepdims=True)
            first = first_ref[k, pair]
            direction = second + beta[None] * first
            by_slot[pair] = (start_ref[k, pair] + alpha[None] * first) + step[None] * direction
        for b in range(SLOTS):
            multipliers_ref[k, b * BLK:(b + 1) * BLK] = by_slot[slot_ref[k, b]]
    norm_ref[...] = jnp.broadcast_to(total[None], norm_ref.shape)


def combine_kernel(dots, swap_ref, length_ref, split_ref, *rest):
    parts, arrived = rest[0:5], rest[5:9]
    extras, (field_ref, terms_ref, line_ref) = rest[9:-3], rest[-3:]
    row = lax.broadcasted_iota(jnp.int32, (BLK, BLK), 0)
    line_ref[...] = jnp.zeros_like(line_ref)
    totals = [jnp.zeros((8, BLK), F32) for _ in dots]
    for k in range(2):
        for f in range(6):
            for c in range(2):
                q = 2 * f + c
                gap = own(parts, k, f, c) - partner(parts, arrived, swap_ref, k, f, c)
                block = jnp.where(row < length_ref[k, q], gap, 0.0)
                field_ref[k, q] = block
                for n, (left, right) in enumerate(dots):
                    a = block if left is None else extras[left][k, q]
                    b = block if right is None else extras[right][k, q]
                    totals[n] = totals[n] + jnp.sum((a * b).reshape(BLK // 8, 8, BLK), axis=0)
        pieces = thirds(field_ref[k].reshape(SLOTS * BLK, BLK))
        one = jnp.dot(split_ref[k], pieces[0], preferred_element_type=F32)
        two = jnp.dot(split_ref[k], pieces[1], preferred_element_type=F32)
        three = jnp.dot(split_ref[k], pieces[2], preferred_element_type=F32)
        terms = one[0:8] + ((one[8:16] + two[0:8]) + ((one[16:24] + two[8:16]) + three[0:8]))
        line_ref[MODES * k:MODES * (k + 1)] = terms[0:MODES]
    for n, total in enumerate(totals):
        line_ref[12 + n:13 + n] = jnp.sum(total, axis=0, keepdims=True)
    terms_ref[...] = jnp.broadcast_to(line_ref[...][None], terms_ref.shape)


def send(parts):
    def moved(value, axis, step):
        count = lax.axis_size(axis)
        return lax.ppermute(value, axis, [(i, (i + step) % count) for i in range(count)])

    sub = ("p", "core")
    return (
        moved(parts[2], "x", 1), moved(parts[1], "x", -1),
        moved(parts[4], sub, 1), moved(parts[3], sub, -1),
    )


def combine(dots, places, swaps, lengths, split, parts, *extras):
    kernel = functools.partial(combine_kernel, dots)
    out = (FIELD, shape(places, ROWS, BLK))
    specs = [SMEM] * 2 + [VMEM] * (10 + len(extras))
    return call(kernel, out, specs, [pltpu.VMEM((ROWS, BLK), F32)])(
        swaps, lengths, split, *parts, *send(parts), *extras
    )


def coarse_table(coarse_inverse, places):
    group = min(places, 8)
    span = group * 8 * MODES * 2
    line = jnp.arange(span, dtype=jnp.int32)[:, None]
    lane = jnp.arange(8 * group * ROWS, dtype=jnp.int32)[None, :]
    inner, spot, kind = lane % ROWS, (lane // ROWS) % group, lane // (ROWS * group)
    pick = jnp.where((line == spot * 96 + kind * 12 + inner) & (inner < 12), 1.0, 0.0).astype(F32)
    sorted_columns = jnp.einsum(
        "rgj,jl->rgl", coarse_inverse.reshape(12, places // group, span), pick, precision=lax.Precision.HIGHEST
    )
    by_kind = sorted_columns.reshape(12, places // group, 8, group * ROWS).transpose(2, 0, 1, 3)
    by_kind = jnp.pad(by_kind.reshape(8, 12, places * ROWS), ((0, 0), (0, 4), (0, 0)))
    here = lax.all_to_all(by_kind, ("core", "x"), 0, 0, tiled=True)
    before = lax.ppermute(here[4:8], "p", [(i, (i + 1) % places) for i in range(places)])
    after = lax.ppermute(here[0:4], "p", [(i, (i - 1) % places) for i in range(places)])
    return tuple(part.reshape(-1, places * ROWS) for part in (before, here, after))


def body(schur, local_gap, modes, rigid_loads, coarse_inverse, slots, swaps, lengths):
    places = lax.axis_size("p")
    loads = jnp.pad(rigid_loads.reshape(2 * MODES, BLK), ((0, 4), (0, 0)))
    loads = jnp.broadcast_to(loads[None], (places, ROWS, BLK))
    table = coarse_table(coarse_inverse, places)
    split, *mode_parts = arrange_modes(slots, modes)
    mode_arrived = send(mode_parts)
    operator_flops = 2 * 2 * SLOTS * BLK * SLOTS * BLK * BLK
    operator_bytes = 2 * SLOTS * BLK * SLOTS * BLK * 2

    partial = coarse_solve(table, loads)
    lift, start, *images = call(
        first_kernel,
        (shape(2, 6, 2 * BLK, 6 * ROWS, kind=BF16), FIELD) + PARTS,
        [SMEM] * 3 + [VMEM] * 2 + [ANY] + [VMEM] * 9,
        SCRATCH, operator_flops, operator_bytes,
    )(slots, swaps, lengths, partial, local_gap, schur, *mode_parts, *mode_arrived)
    residual, terms = combine((), places, swaps, lengths, split, images)

    partial = coarse_solve(table, terms)
    projected, *images = call(
        project_kernel, (FIELD,) + PARTS, [SMEM] + [VMEM] * 2 + [ANY, VMEM], SCRATCH, operator_flops, operator_bytes
    )(slots, partial, lift, schur, residual)
    image, terms = combine(((0, 0), (0, None)), places, swaps, lengths, split, images, projected)

    partial = coarse_solve(table, terms)
    sums, change, second, *images = call(
        step_kernel, (shape(8, BLK), FIELD, FIELD) + PARTS, [SMEM] + [VMEM] * 2 + [ANY] + [VMEM] * 2,
        SCRATCH, operator_flops, operator_bytes,
    )(slots, partial, lift, schur, image, projected)
    dots = ((0, 0), (0, None), (1, None), (0, 2))
    second_image, terms = combine(dots, places, swaps, lengths, split, images, second, projected, image)

    partial = coarse_solve(table, terms)
    multipliers, norm = call(
        last_kernel, (shape(2, SLOTS * BLK, BLK), shape(places, 8, BLK)), [SMEM] + [VMEM] * 8,
        [SCRATCH[0], SCRATCH[3]],
    )(slots, partial, lift, sums, start, projected, change, second, second_image)
    norm = jnp.sum(lax.all_to_all(norm, "p", 0, 0, tiled=True), axis=0)
    norm = lax.all_to_all(jnp.broadcast_to(norm[None], (8, 8, BLK)), ("core", "x"), 0, 0, tiled=True)
    return multipliers, jnp.sqrt(jnp.sum(norm[:, 0], axis=0) / sums[4])


def solution(mesh):
    fine = Mesh(mesh.devices.reshape(-1, 2, 4), ("p", "core", "x"))
    everywhere = ("p", "core", "x")
    deep, flat = P(everywhere, None, None), P(everywhere, None)
    in_specs = (deep, deep, deep, deep, flat, flat, flat, flat)
    return jax.shard_map(body, mesh=fine, in_specs=in_specs, out_specs=(deep, P()), check_vma=False)
```

time: 1000 us -> 244 us (0.24)
  waiting for transfers between devices: 441 us -> 31.1 us
  blocking collectives: 311 us -> 113 us
  local copies, waits for them, and re-layouts: 94.4 us -> 2.7 us
  Pallas kernels: 0 us -> 47 us
  matrix products: 46 us -> 2.78 us
  other arithmetic: 39.2 us -> 0.6 us
  between operations: 14.7 us -> 0.82 us
    all_gather x4 -> x0, waiting for transfers between devices: 409 us -> none  [coarse_apply(): piece = lax.all_gather(terms, ('sub', 'grp'), axis=0, tiled=True)]
    psum x4 -> x0, blocking collectives: 311 us -> none  [the longest x3 237 us: global_norm(): return lax.psum(dual_dot(vector, vector), ('sub', 'grp'))]
    all_to_all x0 -> x8, blocking collectives: none -> 113 us  [the longest x3 45.6 us: coarse_solve(): gathered = lax.all_to_all(terms, 'p', 0, 0, tiled=True)]
    pallas_call x0 -> x12, Pallas kernels: none -> 47 us  [the longest x3 10.5 us: combine(): call(kernel, out, specs, [pltpu.VMEM((ROWS, BLK), F32)])]
    dot_general x14 -> x1, matrix products: 46 us -> 2.78 us  [coarse_table(): jnp.einsum('rgj,jl->rgl', coarse_inverse.reshape(12, places // group, spa...]
    gather x22 -> x0, local copies, waits for them, and re-layouts: 39.6 us -> none  [the longest x8 20.4 us: face_partners(): picked = jnp.take_along_axis(incoming, take_index[:, :, None, None], axis=1)]
    unnamed x59 -> x15, local copies, waits for them, and re-layouts: 25.9 us -> 0.17 us
    ppermute x28 -> x18, starting transfers between devices: 48.5 us -> 23.6 us  [the longest x16 18.9 us: moved(): lax.ppermute(value, axis, [(i, (i + step) % count) for i in range(count)])]
  transfers between devices with their start and end apart: 32 -> 21, of which waited for: 16 -> 12; matrix products, arithmetic and copies ran while one was open for 2% -> 0% of each run, Pallas kernels for 0% -> 0%
where the time goes in v1:
time: 244 us; the launch traced here: 243 us
  blocking collectives  113 us (46%)
  Pallas kernels  47 us (19%)
  starting transfers between devices  45.6 us (19%)
  waiting for transfers between devices  31.1 us (13%)
  matrix products  2.78 us (1%)
  local copies, waits for them, and re-layouts  2.7 us (1%)
    all_to_all x3, blocking collectives, coarse_solve(): gathered = lax.all_to_all(terms, 'p', 0, 0, tiled=True)  45.6 us
    all_to_all x3, blocking collectives, coarse_solve(): return lax.all_to_all(partial, ('core', 'x'), 0, 0, tiled=True)  44.7 us
    ppermute x16, starting transfers between devices, moved(): lax.ppermute(value, axis, [(i, (i + step) % count) for i in range(count)])  18.9 us
    ppermute x16, waiting for transfers between devices, moved(): lax.ppermute(value, axis, [(i, (i + step) % count) for i in range(count)])  15.6 us
    all_to_all x1, blocking collectives, body(): norm = jnp.sum(lax.all_to_all(norm, 'p', 0, 0, tiled=True), axis=0)  13.2 us
    all_to_all x1, starting transfers between devices, coarse_solve(): gathered = lax.all_to_all(terms, 'p', 0, 0, tiled=True)  10.6 us
    pallas_call x3, Pallas kernels, combine(): call(kernel, out, specs, [pltpu.VMEM((ROWS, BLK), F32)])  10.5 us
    pallas_call x1, Pallas kernels, body(): call(step_kernel, (shape(8, BLK), FIELD, FIELD) + PARTS, [SMEM] + [VMEM]...  9.87 us
  transfers between devices with their start and end apart: 21, of which 12 were waited for; matrix products, arithmetic and copies ran while one was open for 0% of the time, Pallas kernels for 0%

profile of v1, /device:TPU:1, one launch (start us, length us, event | category | flops | bytes accessed | tf_op | source)
XLA Modules:
  0.0 243.5 jit_solution(13494012100493393205)
XLA Ops:
  0.7 1.0 reshape.137
  1.7 2.8 %fusion.9 = f32[12,4,1024]{2,0,1:T(8,128)S(1)} fusion(s32[1024]{0:T(1024)S(1)} %fusion.22, pred[1024]{0:T(1024)(128)(4,1)S(1)} %fusion.24, f32[12,4,768]{2,1,0:T(4,128)S(1)} %reshape.137), kind=kOutput, calls=%fused_computation.9 | convolution fusion | flops 455344128 | bytes 349184 | tf_op jit(solution)/shard_map/rgj,jl->rgl/dot_general | solution.py:317
  4.6 0.7 pad.8.clone
  5.4 6.6 %all-to-all-start = ((f32[8,16,512]{2,1,0:T(8,128)}), f32[8,16,512]{2,1,0:T(8,128)S(1)}, u32[]{:S(2)}, u32[]{:S(2)}) async-start(f32[8,16,512]{2,1,0:T(8,128)} %pad.8.clone), calls=%async_computation | async-start | bytes 524288 | tf_op jit(solution)/shard_map/all_to_all | solution.py:322
  12.0 6.5 %all-to-all-done = f32[8,16,512]{2,1,0:T(8,128)S(1)} async-done(((f32[8,16,512]{2,1,0:T(8,128)}), f32[8,16,512]{2,1,0:T(8,128)S(1)}, u32[]{:S(2)}, u32[]{:S(2)}) %all-to-all-start) | async-done | bytes 262176 | tf_op jit(solution)/shard_map/all_to_all | solution.py:322
  18.5 0.7 broadcast_in_dim.24
  19.2 10.6 %all-to-all-start.1 = ((f32[32,16,128]{2,1,0:T(8,128)}), f32[32,16,128]{2,1,0:T(8,128)S(1)}, u32[]{:S(2)}, u32[]{:S(2)}) async-start(f32[32,16,128]{2,1,0:T(8,128)} %broadcast_in_dim.24), calls=%async_computation.1 | async-start | bytes 524288 | tf_op jit(solution)/shard_map/all_to_all | solution.py:111
  29.8 4.7 %collective-permute-start.1 = (f32[4,16,512]{2,1,0:T(8,128)S(1)}, f32[4,16,512]{2,1,0:T(8,128)S(1)}, u32[]{:S(2)}, u32[]{:S(2)}) collective-permute-start(f32[4,16,512]{2,1,0:T(8,128)S(1)} %get-tuple-element.72), channel_id=1, source_target_pairs={{0,248},{8,0},{16,8},{24,16},{32,24},{40,32},{48,40},{56,48},{64,5... | collective-permute-start | bytes 393224 | tf_op jit(solution)/shard_map/ppermute | solution.py:324
  34.6 5.2 %collective-permute-done.1 = f32[4,16,512]{2,1,0:T(8,128)S(1)} collective-permute-done((f32[4,16,512]{2,1,0:T(8,128)S(1)}, f32[4,16,512]{2,1,0:T(8,128)S(1)}, u32[]{:S(2)}, u32[]{:S(2)}) %collective-permute-start.1) | collective-permute-done | bytes 131104 | tf_op jit(solution)/shard_map/ppermute | solution.py:324
  39.8 3.7 %collective-permute-done = f32[4,16,512]{2,1,0:T(8,128)S(1)} collective-permute-done((f32[4,16,512]{2,1,0:T(8,128)S(1)}, f32[4,16,512]{2,1,0:T(8,128)S(1)}, u32[]{:S(2)}, u32[]{:S(2)}) %collective-permute-start) | collective-permute-done | bytes 131104 | tf_op jit(solution)/shard_map/ppermute | solution.py:323
  43.5 1.3 shard_map.96
  44.8 4.9 %all-to-all-start.2 = ((f32[8,5,16,128]{3,2,1,0:T(8,128)}), f32[8,5,16,128]{3,2,1,0:T(8,128)S(1)}, u32[]{:S(2)}, u32[]{:S(2)}) async-start(f32[8,5,16,128]{3,2,1,0:T(8,128)} %shard_map.96), calls=%async_computation.2 | async-start | bytes 655360 | tf_op jit(solution)/shard_map/all_to_all | solution.py:113
  50.3 2.7 %collective-permute-start.3 = (f32[2,2,8,128]{3,2,1,0:T(8,128)S(1)}, f32[2,2,8,128]{3,2,1,0:T(8,128)S(1)}, u32[]{:S(2)}, u32[]{:S(2)}) collective-permute-start(f32[2,2,8,128]{3,2,1,0:T(8,128)S(1)} %get-tuple-element.39.rest_1_), channel_id=1, source_target_pairs={{0,3},{1,0},{2,1},{3,2},{4,7},{5,4},{6,5},{7,6},{8,11},{9,8},{10,9... | collective-permute-start | bytes 49160 | tf_op jit(solution)/shard_map/ppermute | solution.py:292
  53.0 0.6 collective-permute-start.5
  53.6 1.1 collective-permute-start.4
  54.7 1.1 collective-permute-done.3.rest_6_
  55.9 1.2 collective-permute-done.2.rest_5_
  57.1 9.1 %shard_map.97 = (bf16[2,6,256,96]{3,2,1,0:T(8,128)(2,1)S(1)}, f32[2,12,128,128]{3,2,1,0:T(8,128)}, f32[2,4,128,128]{3,2,1,0:T(8,128)S(1)}, f32[2,2,128,128]{3,2,...) custom-call(s32[2,12]{1,0:T(2,128)S(1)} %copy-done.1, ...), custom_call_target="tpu_custom_call" | custom-call | flops 1207959552 | bytes 9437184 | tf_op jit(solution)/shard_map/pallas_call | solution.py:339
  66.2 2.0 collective-permute-start.7
  68.2 4.8 %collective-permute-start.9 = (f32[2,2,128,128]{3,2,1,0:T(8,128)S(1)}, f32[2,2,128,128]{3,2,1,0:T(8,128)S(1)}, u32[]{:S(2)}, u32[]{:S(2)}) collective-permute-start(f32[2,2,128,128]{3,2,1,0:T(8,128)S(1)} %get-tuple-element.46.rest_3_), channel_id=1, source_target_pairs={{0,252},{4,0},{8,4},{12,8},{16,12},{20,16},{24,20},{28,24},{32,28}... | collective-permute-start | bytes 786440 | tf_op jit(solution)/shard_map/ppermute | solution.py:292
  73.0 1.7 collective-permute-done.6.rest_5_
  74.7 1.7 collective-permute-done.8.rest_7_
  76.3 2.4 shard_map.98
  78.7 16.5 %all_to_all.55.terms_ref = f32[32,16,128]{2,1,0:T(8,128)S(1)} all-to-all(f32[32,16,128]{2,1,0:T(8,128)S(1)} %get-tuple-element.48), channel_id=1, replica_groups=mesh['p'=32,'core'=2,'x'=4] {'p'}, dimensions={0} | all-to-all | bytes 524288 | tf_op jit(solution)/shard_map/all_to_all | solution.py:111
  95.9 15.5 %all_to_all.56.partial_ref = f32[8,5,16,128]{3,2,1,0:T(8,128)S(1)} all-to-all(f32[8,5,16,128]{3,2,1,0:T(8,128)S(1)} %shard_map.99), channel_id=1, replica_groups=mesh['p'=32,'core'=2,'x'=4] {'core','x'}, dimensions={0} | all-to-all | bytes 655360 | tf_op jit(solution)/shard_map/all_to_all | solution.py:113
  111.4 8.9 %shard_map.100 = (f32[2,12,128,128]{3,2,1,0:T(8,128)}, f32[2,4,128,128]{3,2,1,0:T(8,128)S(1)}, f32[2,2,128,128]{3,2,1,0:T(8,128)S(1)}, f32[2,2,128,128]{3,2,1,0:...) custom-call(s32[2,12]{1,0:T(2,128)S(1)} %copy-done.1, ...), custom_call_target="tpu_custom_call" | custom-call | flops 1207959552 | bytes 9437184 | tf_op jit(solution)/shard_map/pallas_call | solution.py:348
  120.3 0.9 collective-permute-start.11
  121.2 0.7 collective-permute-start.10
  121.8 1.0 collective-permute-start.13
  122.8 1.3 collective-permute-start.12
  124.2 3.7 %collective-permute-done.11.rest_6_ = f32[2,2,128,128]{3,2,1,0:T(8,128)S(1)} collective-permute-done((f32[2,2,128,128]{3,2,1,0:T(8,128)S(1)}, f32[2,2,128,128]{3,2,1,0:T(8,128)S(1)}, u32[]{:S(2)}, u32[]{:S(2)}) %collective-permute-start.11) | collective-permute-done | bytes 262176 | tf_op jit(solution)/shard_map/ppermute | solution.py:292
  127.9 1.3 collective-permute-done.10.rest_5_
  129.2 3.5 %shard_map.101 = (f32[2,12,128,128]{3,2,1,0:T(8,128)}, f32[32,16,128]{2,1,0:T(8,128)S(1)}) custom-call(s32[2,6]{1,0:T(2,128)S(1)} %copy-done.2, s32[2,12]{1,0:T(2,128)S(1)} %copy-done.3, bf16[2,32,1536]{2,1,0:T(8,128)(2,1)S(1)} %get-tuple-element.37.split_ref, f32[2,4,128,128]{3,2,1,0:T(8,128)S(1)} %get-tuple-element.51.rest_0_, ...), custom_call_target="tpu_custom_call" | custom-call | tf_op jit(solution)/shard_map/pallas_call | solution.py:305
  132.7 14.5 %all_to_all.57.terms_ref = f32[32,16,128]{2,1,0:T(8,128)S(1)} all-to-all(f32[32,16,128]{2,1,0:T(8,128)S(1)} %get-tuple-element.57), channel_id=1, replica_groups=mesh['p'=32,'core'=2,'x'=4] {'p'}, dimensions={0} | all-to-all | bytes 524288 | tf_op jit(solution)/shard_map/all_to_all | solution.py:111
  147.7 14.6 %all_to_all.58.partial_ref = f32[8,5,16,128]{3,2,1,0:T(8,128)S(1)} all-to-all(f32[8,5,16,128]{3,2,1,0:T(8,128)S(1)} %shard_map.102), channel_id=1, replica_groups=mesh['p'=32,'core'=2,'x'=4] {'core','x'}, dimensions={0} | all-to-all | bytes 655360 | tf_op jit(solution)/shard_map/all_to_all | solution.py:113
  162.3 9.9 %shard_map.103 = (f32[8,128]{1,0:T(8,128)S(1)}, f32[2,12,128,128]{3,2,1,0:T(8,128)}, f32[2,12,128,128]{3,2,1,0:T(8,128)}, f32[2,4,128,128]{3,2,1,0:T(8,128)S(1)}...) custom-call(s32[2,12]{1,0:T(2,128)S(1)} %copy-done.1, ...), custom_call_target="tpu_custom_call" | custom-call | flops 1207959552 | bytes 9437184 | tf_op jit(solution)/shard_map/pallas_call | solution.py:354
  172.2 0.9 collective-permute-start.15
  173.1 0.7 collective-permute-start.14
  173.8 1.0 collective-permute-start.17
  174.7 1.3 collective-permute-start.16
  176.0 3.8 %collective-permute-done.15.rest_6_ = f32[2,2,128,128]{3,2,1,0:T(8,128)S(1)} collective-permute-done((f32[2,2,128,128]{3,2,1,0:T(8,128)S(1)}, f32[2,2,128,128]{3,2,1,0:T(8,128)S(1)}, u32[]{:S(2)}, u32[]{:S(2)}) %collective-permute-start.15) | collective-permute-done | bytes 262176 | tf_op jit(solution)/shard_map/ppermute | solution.py:292
  179.8 1.3 collective-permute-done.14.rest_5_
  181.1 4.5 %shard_map.104 = (f32[2,12,128,128]{3,2,1,0:T(8,128)}, f32[32,16,128]{2,1,0:T(8,128)S(1)}) custom-call(s32[2,6]{1,0:T(2,128)S(1)} %copy-done.2, s32[2,12]{1,0:T(2,128)S(1)} %copy-done.3, bf16[2,32,1536]{2,1,0:T(8,128)(2,1)S(1)} %get-tuple-element.37.split_ref, f32[2,4,128,128]{3,2,1,0:T(8,128)S(1)} %get-tuple-element.59.rest_0_, ...), custom_call_target="tpu_custom_call" | custom-call | tf_op jit(solution)/shard_map/pallas_call | solution.py:305
  185.6 14.6 %all_to_all.59.terms_ref = f32[32,16,128]{2,1,0:T(8,128)S(1)} all-to-all(f32[32,16,128]{2,1,0:T(8,128)S(1)} %get-tuple-element.65), channel_id=1, replica_groups=mesh['p'=32,'core'=2,'x'=4] {'p'}, dimensions={0} | all-to-all | bytes 524288 | tf_op jit(solution)/shard_map/all_to_all | solution.py:111
  200.8 14.6 %all_to_all.60.partial_ref = f32[8,5,16,128]{3,2,1,0:T(8,128)S(1)} all-to-all(f32[8,5,16,128]{3,2,1,0:T(8,128)S(1)} %shard_map.105), channel_id=1, replica_groups=mesh['p'=32,'core'=2,'x'=4] {'core','x'}, dimensions={0} | all-to-all | bytes 655360 | tf_op jit(solution)/shard_map/all_to_all | solution.py:113
  215.4 5.0 %shard_map.106 = (f32[2,1536,128]{2,1,0:T(8,128)}, f32[32,8,128]{2,1,0:T(8,128)S(1)}) custom-call(s32[2,12]{1,0:T(2,128)S(1)} %copy-done.1, f32[8,5,16,128]{3,2,1,0:T(8,128)S(1)} %all_to_all.60.partial_ref, bf16[2,6,256,96]{3,2,1,0:T(8,128)(2,1)S(1)} %get-tuple-element.49.lift_ref, f32[8,128]{1,0:T(8,128)S(1)} %get-tuple-element.66.sums_ref, ...), custom_call_target="tpu_custom_call" | custom-call | tf_op jit(solution)/shard_map/pallas_call | solution.py:362
  220.3 13.2 %all_to_all.61 = f32[32,8,128]{2,1,0:T(8,128)S(1)} all-to-all(f32[32,8,128]{2,1,0:T(8,128)S(1)} %get-tuple-element.71), channel_id=1, replica_groups=mesh['p'=32,'core'=2,'x'=4] {'p'}, dimensions={0} | all-to-all | bytes 262144 | tf_op jit(solution)/shard_map/all_to_all | solution.py:366
  233.6 9.4 %all_to_all.62 = f32[8,8,128]{2,1,0:T(8,128)S(1)} all-to-all(f32[8,8,128]{2,1,0:T(8,128)S(1)} %broadcast_in_dim.25), channel_id=1, replica_groups=mesh['p'=32,'core'=2,'x'=4] {'core','x'}, dimensions={0} | all-to-all | bytes 65536 | tf_op jit(solution)/shard_map/all_to_all | solution.py:367
  (45 shorter events, 3.3 us)
Async XLA Ops:
  4.4 7.5 %copy-start.5 = (f32[2,6,128]{2,0,1:T(2,128)S(1)}, f32[2,6,128]{2,0,1:T(2,128)}, u32[]{:S(2)}) copy-start(f32[2,6,128]{2,0,1:T(2,128)} %param.11) | copy-start | bytes 18436
  5.4 13.1 %all-to-all-start = ((f32[8,16,512]{2,1,0:T(8,128)}), f32[8,16,512]{2,1,0:T(8,128)S(1)}, u32[]{:S(2)}, u32[]{:S(2)}) async-start(f32[8,16,512]{2,1,0:T(8,128)} %pad.8.clone), calls=%async_computation | async-start | bytes 524288 | tf_op jit(solution)/shard_map/all_to_all | solution.py:322
  11.9 37.7 %copy-start.4 = (f32[2,6,1536]{2,0,1:T(2,128)S(1)}, f32[2,6,1536]{2,0,1:T(2,128)}, u32[]{:S(2)}) copy-start(f32[2,6,1536]{2,0,1:T(2,128)} %param.10) | copy-start | bytes 221188
  12.0 37.7 %copy-start.1 = (s32[2,12]{1,0:T(2,128)S(1)}, s32[2,12]{1,0:T(2,128)}, u32[]{:S(2)}) copy-start(s32[2,12]{1,0:T(2,128)} %slot_ref.9) | copy-start | bytes 292
  19.2 37.9 %copy-start.2 = (s32[2,6]{1,0:T(2,128)S(1)}, s32[2,6]{1,0:T(2,128)}, u32[]{:S(2)}) copy-start(s32[2,6]{1,0:T(2,128)} %swap_ref.7) | copy-start | bytes 148
  19.2 37.9 %copy-start.3 = (s32[2,12]{1,0:T(2,128)S(1)}, s32[2,12]{1,0:T(2,128)}, u32[]{:S(2)}) copy-start(s32[2,12]{1,0:T(2,128)} %length_ref.7) | copy-start | bytes 292
  19.2 24.2 %all-to-all-start.1 = ((f32[32,16,128]{2,1,0:T(8,128)}), f32[32,16,128]{2,1,0:T(8,128)S(1)}, u32[]{:S(2)}, u32[]{:S(2)}) async-start(f32[32,16,128]{2,1,0:T(8,128)} %broadcast_in_dim.24), calls=%async_computation.1 | async-start | bytes 524288 | tf_op jit(solution)/shard_map/all_to_all | solution.py:111
  29.8 10.0 %collective-permute-start.1 = (f32[4,16,512]{2,1,0:T(8,128)S(1)}, f32[4,16,512]{2,1,0:T(8,128)S(1)}, u32[]{:S(2)}, u32[]{:S(2)}) collective-permute-start(f32[4,16,512]{2,1,0:T(8,128)S(1)} %get-tuple-element.72), channel_id=1, source_target_pairs={{0,248},{8,0},{16,8},{24,16},{32,24},{40,32},{48,40},{56,48},{64,5... | collective-permute-start | bytes 393224 | tf_op jit(solution)/shard_map/ppermute | solution.py:324
  34.5 8.9 %collective-permute-start = (f32[4,16,512]{2,1,0:T(8,128)S(1)}, f32[4,16,512]{2,1,0:T(8,128)S(1)}, u32[]{:S(2)}, u32[]{:S(2)}) collective-permute-start(f32[4,16,512]{2,1,0:T(8,128)S(1)} %get-tuple-element.73), channel_id=1, source_target_pairs={{0,8},{8,16},{16,24},{24,32},{32,40},{40,48},{48,56},{56,64},{64,7... | collective-permute-start | bytes 393224 | tf_op jit(solution)/shard_map/ppermute | solution.py:323
  44.8 12.3 %all-to-all-start.2 = ((f32[8,5,16,128]{3,2,1,0:T(8,128)}), f32[8,5,16,128]{3,2,1,0:T(8,128)S(1)}, u32[]{:S(2)}, u32[]{:S(2)}) async-start(f32[8,5,16,128]{3,2,1,0:T(8,128)} %shard_map.96), calls=%async_computation.2 | async-start | bytes 655360 | tf_op jit(solution)/shard_map/all_to_all | solution.py:113
  50.3 5.6 %collective-permute-start.3 = (f32[2,2,8,128]{3,2,1,0:T(8,128)S(1)}, f32[2,2,8,128]{3,2,1,0:T(8,128)S(1)}, u32[]{:S(2)}, u32[]{:S(2)}) collective-permute-start(f32[2,2,8,128]{3,2,1,0:T(8,128)S(1)} %get-tuple-element.39.rest_1_), channel_id=1, source_target_pairs={{0,3},{1,0},{2,1},{3,2},{4,7},{5,4},{6,5},{7,6},{8,11},{9,8},{10,9... | collective-permute-start | bytes 49160 | tf_op jit(solution)/shard_map/ppermute | solution.py:292
  53.0 4.0 %collective-permute-start.2 = (f32[2,2,8,128]{3,2,1,0:T(8,128)S(1)}, f32[2,2,8,128]{3,2,1,0:T(8,128)S(1)}, u32[]{:S(2)}, u32[]{:S(2)}) collective-permute-start(f32[2,2,8,128]{3,2,1,0:T(8,128)S(1)} %get-tuple-element.40.rest_2_), channel_id=1, source_target_pairs={{0,1},{1,2},{2,3},{3,0},{4,5},{5,6},{6,7},{7,4},{8,9},{9,10},{10,1... | collective-permute-start | bytes 49160 | tf_op jit(solution)/shard_map/ppermute | solution.py:292
  53.0 4.0 %collective-permute-start.5 = (f32[2,2,8,128]{3,2,1,0:T(8,128)S(1)}, f32[2,2,8,128]{3,2,1,0:T(8,128)S(1)}, u32[]{:S(2)}, u32[]{:S(2)}) collective-permute-start(f32[2,2,8,128]{3,2,1,0:T(8,128)S(1)} %get-tuple-element.41.rest_3_), channel_id=1, source_target_pairs={{0,252},{4,0},{8,4},{12,8},{16,12},{20,16},{24,20},{28,24},{32,28}... | collective-permute-start | bytes 49160 | tf_op jit(solution)/shard_map/ppermute | solution.py:292
  53.6 3.4 %collective-permute-start.4 = (f32[2,2,8,128]{3,2,1,0:T(8,128)S(1)}, f32[2,2,8,128]{3,2,1,0:T(8,128)S(1)}, u32[]{:S(2)}, u32[]{:S(2)}) collective-permute-start(f32[2,2,8,128]{3,2,1,0:T(8,128)S(1)} %get-tuple-element.42.rest_4_), channel_id=1, source_target_pairs={{0,4},{4,8},{8,12},{12,16},{16,20},{20,24},{24,28},{28,32},{32,36}... | collective-permute-start | bytes 49160 | tf_op jit(solution)/shard_map/ppermute | solution.py:292
  66.2 6.8 %collective-permute-start.7 = (f32[2,2,128,128]{3,2,1,0:T(8,128)S(1)}, f32[2,2,128,128]{3,2,1,0:T(8,128)S(1)}, u32[]{:S(2)}, u32[]{:S(2)}) collective-permute-start(f32[2,2,128,128]{3,2,1,0:T(8,128)S(1)} %get-tuple-element.44.rest_1_), channel_id=1, source_target_pairs={{0,3},{1,0},{2,1},{3,2},{4,7},{5,4},{6,5},{7,6},{8,11},{9,8},{10,9... | collective-permute-start | bytes 786440 | tf_op jit(solution)/shard_map/ppermute | solution.py:292
  68.2 6.4 %collective-permute-start.6 = (f32[2,2,128,128]{3,2,1,0:T(8,128)S(1)}, f32[2,2,128,128]{3,2,1,0:T(8,128)S(1)}, u32[]{:S(2)}, u32[]{:S(2)}) collective-permute-start(f32[2,2,128,128]{3,2,1,0:T(8,128)S(1)} %get-tuple-element.45.rest_2_), channel_id=1, source_target_pairs={{0,1},{1,2},{2,3},{3,0},{4,5},{5,6},{6,7},{7,4},{8,9},{9,10},{10,1... | collective-permute-start | bytes 786440 | tf_op jit(solution)/shard_map/ppermute | solution.py:292
  68.2 6.4 %collective-permute-start.9 = (f32[2,2,128,128]{3,2,1,0:T(8,128)S(1)}, f32[2,2,128,128]{3,2,1,0:T(8,128)S(1)}, u32[]{:S(2)}, u32[]{:S(2)}) collective-permute-start(f32[2,2,128,128]{3,2,1,0:T(8,128)S(1)} %get-tuple-element.46.rest_3_), channel_id=1, source_target_pairs={{0,252},{4,0},{8,4},{12,8},{16,12},{20,16},{24,20},{28,24},{32,28}... | collective-permute-start | bytes 786440 | tf_op jit(solution)/shard_map/ppermute | solution.py:292
  73.0 3.3 %collective-permute-start.8 = (f32[2,2,128,128]{3,2,1,0:T(8,128)S(1)}, f32[2,2,128,128]{3,2,1,0:T(8,128)S(1)}, u32[]{:S(2)}, u32[]{:S(2)}) collective-permute-start(f32[2,2,128,128]{3,2,1,0:T(8,128)S(1)} %get-tuple-element.47.rest_4_), channel_id=1, source_target_pairs={{0,4},{4,8},{8,12},{12,16},{16,20},{20,24},{24,28},{28,32},{32,36}... | collective-permute-start | bytes 786440 | tf_op jit(solution)/shard_map/ppermute | solution.py:292
  120.3 7.6 %collective-permute-start.11 = (f32[2,2,128,128]{3,2,1,0:T(8,128)S(1)}, f32[2,2,128,128]{3,2,1,0:T(8,128)S(1)}, u32[]{:S(2)}, u32[]{:S(2)}) collective-permute-start(f32[2,2,128,128]{3,2,1,0:T(8,128)S(1)} %get-tuple-element.52.rest_1_), channel_id=1, source_target_pairs={{0,3},{1,0},{2,1},{3,2},{4,7},{5,4},{6,5},{7,6},{8,11},{9,8},{10,9... | collective-permute-start | bytes 786440 | tf_op jit(solution)/shard_map/ppermute | solution.py:292
  121.2 8.0 %collective-permute-start.10 = (f32[2,2,128,128]{3,2,1,0:T(8,128)S(1)}, f32[2,2,128,128]{3,2,1,0:T(8,128)S(1)}, u32[]{:S(2)}, u32[]{:S(2)}) collective-permute-start(f32[2,2,128,128]{3,2,1,0:T(8,128)S(1)} %get-tuple-element.53.rest_2_), channel_id=1, source_target_pairs={{0,1},{1,2},{2,3},{3,0},{4,5},{5,6},{6,7},{7,4},{8,9},{9,10},{10,1... | collective-permute-start | bytes 786440 | tf_op jit(solution)/shard_map/ppermute | solution.py:292
  121.8 7.3 %collective-permute-start.13 = (f32[2,2,128,128]{3,2,1,0:T(8,128)S(1)}, f32[2,2,128,128]{3,2,1,0:T(8,128)S(1)}, u32[]{:S(2)}, u32[]{:S(2)}) collective-permute-start(f32[2,2,128,128]{3,2,1,0:T(8,128)S(1)} %get-tuple-element.54.rest_3_), channel_id=1, source_target_pairs={{0,252},{4,0},{8,4},{12,8},{16,12},{20,16},{24,20},{28,24},{32,28}... | collective-permute-start | bytes 786440 | tf_op jit(solution)/shard_map/ppermute | solution.py:292
  122.8 6.4 %collective-permute-start.12 = (f32[2,2,128,128]{3,2,1,0:T(8,128)S(1)}, f32[2,2,128,128]{3,2,1,0:T(8,128)S(1)}, u32[]{:S(2)}, u32[]{:S(2)}) collective-permute-start(f32[2,2,128,128]{3,2,1,0:T(8,128)S(1)} %get-tuple-element.55.rest_4_), channel_id=1, source_target_pairs={{0,4},{4,8},{8,12},{12,16},{16,20},{20,24},{24,28},{28,32},{32,36}... | collective-permute-start | bytes 786440 | tf_op jit(solution)/shard_map/ppermute | solution.py:292
  172.2 7.6 %collective-permute-start.15 = (f32[2,2,128,128]{3,2,1,0:T(8,128)S(1)}, f32[2,2,128,128]{3,2,1,0:T(8,128)S(1)}, u32[]{:S(2)}, u32[]{:S(2)}) collective-permute-start(f32[2,2,128,128]{3,2,1,0:T(8,128)S(1)} %get-tuple-element.60.rest_1_), channel_id=1, source_target_pairs={{0,3},{1,0},{2,1},{3,2},{4,7},{5,4},{6,5},{7,6},{8,11},{9,8},{10,9... | collective-permute-start | bytes 786440 | tf_op jit(solution)/shard_map/ppermute | solution.py:292
  173.1 8.0 %collective-permute-start.14 = (f32[2,2,128,128]{3,2,1,0:T(8,128)S(1)}, f32[2,2,128,128]{3,2,1,0:T(8,128)S(1)}, u32[]{:S(2)}, u32[]{:S(2)}) collective-permute-start(f32[2,2,128,128]{3,2,1,0:T(8,128)S(1)} %get-tuple-element.61.rest_2_), channel_id=1, source_target_pairs={{0,1},{1,2},{2,3},{3,0},{4,5},{5,6},{6,7},{7,4},{8,9},{9,10},{10,1... | collective-permute-start | bytes 786440 | tf_op jit(solution)/shard_map/ppermute | solution.py:292
  173.8 7.3 %collective-permute-start.17 = (f32[2,2,128,128]{3,2,1,0:T(8,128)S(1)}, f32[2,2,128,128]{3,2,1,0:T(8,128)S(1)}, u32[]{:S(2)}, u32[]{:S(2)}) collective-permute-start(f32[2,2,128,128]{3,2,1,0:T(8,128)S(1)} %get-tuple-element.62.rest_3_), channel_id=1, source_target_pairs={{0,252},{4,0},{8,4},{12,8},{16,12},{20,16},{24,20},{28,24},{32,28}... | collective-permute-start | bytes 786440 | tf_op jit(solution)/shard_map/ppermute | solution.py:292
  174.7 6.4 %collective-permute-start.16 = (f32[2,2,128,128]{3,2,1,0:T(8,128)S(1)}, f32[2,2,128,128]{3,2,1,0:T(8,128)S(1)}, u32[]{:S(2)}, u32[]{:S(2)}) collective-permute-start(f32[2,2,128,128]{3,2,1,0:T(8,128)S(1)} %get-tuple-element.63.rest_4_), channel_id=1, source_target_pairs={{0,4},{4,8},{8,12},{12,16},{16,20},{20,24},{24,28},{28,32},{32,36}... | collective-permute-start | bytes 786440 | tf_op jit(solution)/shard_map/ppermute | solution.py:292
  185.6 29.7 %copy-start = (f32[2,12,128,128]{3,2,1,0:T(8,128)S(1)}, f32[2,12,128,128]{3,2,1,0:T(8,128)}, u32[]{:S(2)}) copy-start(f32[2,12,128,128]{3,2,1,0:T(8,128)} %get-tuple-element.67.start_ref) | copy-start | bytes 4718596

commit v2 on v1

v2 whole, which is shorter than its diff:
```python
import functools

import jax
import jax.numpy as jnp
from jax import lax
from jax.experimental import pallas as pl
from jax.experimental.pallas import tpu as pltpu
from jax.sharding import Mesh, PartitionSpec as P

BLK = 128
SLOTS = 12
MODES = 6
ROWS = 16
SPLIT_LEFT = (0, 0, 1, 0, 1, 2)
SPLIT_RIGHT = (0, 1, 0, 2, 1, 0)
F32 = jnp.float32
BF16 = jnp.bfloat16
VMEM = pl.BlockSpec(memory_space=pltpu.VMEM)
SMEM = pl.BlockSpec(memory_space=pltpu.SMEM)


def shape(*dims, kind=F32):
    return jax.ShapeDtypeStruct(dims, kind)


def call(kernel, out, in_specs, scratch=(), flops=0, moved=0):
    return pl.pallas_call(
        kernel,
        out_shape=out,
        in_specs=in_specs,
        out_specs=jax.tree.map(lambda _: VMEM, out),
        scratch_shapes=list(scratch),
        compiler_params=pltpu.CompilerParams(vmem_limit_bytes=24 * 2**20),
        cost_estimate=pl.CostEstimate(flops=flops, bytes_accessed=moved, transcendentals=0),
    )


def thirds(value):
    first = value.astype(BF16)
    rest = value - first.astype(F32)
    second = rest.astype(BF16)
    third = (rest - second.astype(F32)).astype(BF16)
    return first, second, third


def pack_kernel(slot_ref, modes_ref, loads_ref, coarse_ref, split_ref, payload_ref, *rest):
    parts, (by_slot, rows, line) = rest[:5], rest[5:]
    by_slot[...] = jnp.zeros_like(by_slot)
    for k in range(2):
        for b in range(SLOTS):
            for i in range(MODES):
                by_slot[k, slot_ref[k, b], i:i + 1] = modes_ref[i, k:k + 1, b * BLK:(b + 1) * BLK]
    parts[0][...] = by_slot[:, 0:4]
    for n in range(4):
        parts[n + 1][...] = by_slot[:, 4 + 2 * n:6 + 2 * n]
    rows[...] = jnp.zeros_like(rows)
    rows[0:12] = coarse_ref[...]
    line[...] = jnp.zeros_like(line)
    for k in range(2):
        for i in range(MODES):
            line[k * MODES + i:k * MODES + i + 1] = loads_ref[i, k:k + 1]
    places, tiles = payload_ref.shape[0], rows.shape[1] // BLK
    left = lax.broadcasted_iota(jnp.int32, (MODES, BLK), 1) < 64
    for p in range(places):
        first = (96 * p - 48) % (96 * places)
        tile, shift = first // BLK, first % BLK
        wide = [rows[:, (tile + j) % tiles * BLK:((tile + j) % tiles + 1) * BLK] for j in range(3)]
        window = pltpu.roll(jnp.concatenate(wide, axis=1), 3 * BLK - shift, axis=1)
        tail = window[:, BLK:2 * BLK]
        payload_ref[p, 0:12] = window[0:12, 0:BLK]
        payload_ref[p, 12:18] = jnp.where(left, tail[0:6], pltpu.roll(tail, 64, axis=1)[6:12])
        payload_ref[p, 18:32] = line[0:14]
    for k in range(2):
        for q in range(SLOTS):
            pieces = [piece.astype(F32) for piece in thirds(by_slot[k, q])]
            pieces.append(jnp.zeros_like(pieces[0]))
            split_ref[k, :, q * BLK:(q + 1) * BLK] = jnp.concatenate(pieces, axis=0).astype(BF16)


def pack(slots, modes, loads, coarse_inverse, places):
    return call(
        pack_kernel,
        (shape(2, 32, SLOTS * BLK, kind=BF16), shape(places, 32, BLK), shape(2, 4, 8, BLK))
        + (shape(2, 2, 8, BLK),) * 4,
        [SMEM] + [VMEM] * 3,
        [pltpu.VMEM((2, SLOTS, 8, BLK), F32), pltpu.VMEM((ROWS, 96 * places), F32), pltpu.VMEM((ROWS, BLK), F32)],
    )(slots, modes.transpose(1, 0, 2), loads.transpose(1, 0, 2), coarse_inverse)


def partner(parts, arrived, swap_ref, k, f, c):
    meets = jnp.bitwise_xor(swap_ref[k, f], c)
    if f == 0:
        return parts[0][1 - k, 2 + meets]
    if f == 1:
        return parts[0][1 - k, meets]
    return arrived[f - 2][k, meets]


def own(parts, k, f, c):
    return parts[0][k, 2 * f + c] if f < 2 else parts[f - 1][k, c]


def share(core, table, terms, riders, mine_ref, other_ref, solved):
    result = jnp.dot(table, terms, precision=lax.Precision.HIGHEST, preferred_element_type=F32)
    for n in range(4):
        for x in range(4):
            solved[n, x, 0:12] = result[(4 * n + x) * 12:(4 * n + x + 1) * 12]
    for out_ref, c in ((mine_ref, core), (other_ref, 1 - core)):
        for x in range(4):
            out_ref[x, 0:12] = solved[c + 1, x, 0:12]
            out_ref[x, 12:16] = riders
            out_ref[x, 16:28] = solved[c + 1, max(x - 1, 0), 0:12]
            out_ref[x, 28:40] = solved[c + 1, min(x + 1, 3), 0:12]
            out_ref[x, 40:52] = solved[c, x, 0:12]
            out_ref[x, 52:64] = solved[c + 2, x, 0:12]


def partial_kernel(core_ref, table_ref, terms_ref, mine_ref, other_ref, solved):
    riders = jnp.sum(terms_ref[:, 8:16], axis=0)[4:8]
    share(core_ref[0], table_ref[...], terms_ref[...].reshape(-1, BLK), riders, mine_ref, other_ref, solved)


def unpack_kernel(core_ref, swap_ref, length_ref, payload_ref, *rest):
    parts, arrived = rest[0:5], rest[5:9]
    table_ref, lift_ref, mine_ref, other_ref, wide, terms, solved = rest[9:]
    places = payload_ref.shape[0]
    terms[...] = jnp.zeros_like(terms)
    wide[...] = jnp.zeros_like(wide)
    for p in range(places):
        tail = payload_ref[p, 12:18]
        wide[ROWS * p:ROWS * p + 12, 0:BLK] = payload_ref[p, 0:12]
        wide[ROWS * p:ROWS * p + 6, BLK:2 * BLK] = tail
        wide[ROWS * p + 6:ROWS * p + 12, BLK:2 * BLK] = pltpu.roll(tail, 64, axis=1)
        terms[ROWS * p:ROWS * p + 12] = payload_ref[p, 18:30]
    table_ref[...] = wide[...].T[0:192]
    riders = jnp.zeros((4, BLK), F32)
    share(core_ref[0], table_ref[...], terms[...], riders, mine_ref, other_ref, solved)
    lane = lax.broadcasted_iota(jnp.int32, (8, BLK), 1)
    for k in range(2):
        for f in range(6):
            for c in range(2):
                live = lane < length_ref[k, 2 * f + c]
                mine = jnp.where(live, own(parts, k, f, c), 0.0)
                theirs = jnp.where(live, -partner(parts, arrived, swap_ref, k, f, c), 0.0)
                both = jnp.concatenate([mine[0:MODES], theirs[0:MODES], mine[MODES:8], mine[MODES:8]], axis=0)
                pieces = [piece.astype(F32) for piece in thirds(both)]
                left = jnp.concatenate([pieces[n] for n in SPLIT_LEFT], axis=0)
                lift_ref[k, f, c * BLK:(c + 1) * BLK] = left.T.astype(BF16)


SHARES = (shape(4, 64, BLK), shape(4, 64, BLK))
SOLVED = pltpu.VMEM((4, 4, ROWS, BLK), F32)


def unpack(core, swaps, lengths, payload, parts):
    places = payload.shape[0]
    payload = lax.all_to_all(payload, "p", 0, 0, tiled=True)
    return call(
        unpack_kernel,
        (shape(192, places * ROWS), shape(2, 6, 2 * BLK, 6 * ROWS, kind=BF16)) + SHARES,
        [SMEM] * 3 + [VMEM] * 10,
        [pltpu.VMEM((places * ROWS, 2 * BLK), F32), pltpu.VMEM((places * ROWS, BLK), F32), SOLVED],
    )(core, swaps, lengths, payload, *parts, *send(parts))


def collect(mine, other):
    both = mine + lax.ppermute(other, "core", [(0, 1), (1, 0)])
    return lax.all_to_all(both, "x", 0, 0, tiled=True)


def coarse_solve(core, table, terms):
    gathered = lax.all_to_all(terms, "p", 0, 0, tiled=True)
    return collect(*call(partial_kernel, SHARES, [SMEM] + [VMEM] * 2, [SOLVED])(core, table, gathered))


def load_coefficients(partial_ref, coef_ref):
    solved = jnp.sum(partial_ref[...], axis=0)
    coef_ref[...] = jnp.zeros_like(coef_ref)
    for k in range(2):
        other = MODES * (1 - k)
        firsts = [other, other] + [16 + 12 * n + MODES * k for n in range(4)]
        for f in range(6):
            coef_ref[k, f, 0:MODES] = solved[MODES * k:MODES * (k + 1)]
            coef_ref[k, f, MODES:2 * MODES] = solved[firsts[f]:firsts[f] + MODES]
    return solved[0:16]


def lifted(lift_ref, coef_ref, k, f):
    pieces = thirds(coef_ref[k, f])
    right = jnp.concatenate([pieces[n] for n in SPLIT_RIGHT], axis=0)
    return jnp.dot(lift_ref[k, f], right, preferred_element_type=F32)


def apply_schur(schur_ref, rounded, slot_ref, by_slot, parts, base=None):
    for k in range(2):
        for n in range(3):
            image = jnp.dot(schur_ref[k, n * 512:(n + 1) * 512], rounded[k], preferred_element_type=F32)
            for j in range(4):
                b = 4 * n + j
                piece = image[j * BLK:(j + 1) * BLK]
                if base is not None:
                    piece = base[k, b * BLK:(b + 1) * BLK] - piece
                by_slot[slot_ref[k, b]] = piece
        parts[0][k] = by_slot[0:4]
        for n in range(4):
            parts[n + 1][k] = by_slot[4 + 2 * n:6 + 2 * n]


def round_blocks(field_ref, slot_ref, rounded):
    for k in range(2):
        for b in range(SLOTS):
            rounded[k, b * BLK:(b + 1) * BLK] = field_ref[k, slot_ref[k, b]].astype(BF16)


PARTS = (shape(2, 4, BLK, BLK),) + (shape(2, 2, BLK, BLK),) * 4
FIELD = shape(2, SLOTS, BLK, BLK)
SCRATCH = [
    pltpu.VMEM((2, 6, ROWS, BLK), F32),
    pltpu.VMEM((2, SLOTS * BLK, BLK), BF16),
    pltpu.VMEM((SLOTS, BLK, BLK), F32),
]


def first_kernel(slot_ref, partial_ref, lift_ref, schur_ref, gap_ref, *rest):
    field_ref, images = rest[0], rest[1:6]
    coef_ref, rounded, by_slot = rest[6:]
    load_coefficients(partial_ref, coef_ref)
    for k in range(2):
        for f in range(6):
            field_ref[k, 2 * f:2 * f + 2] = lifted(lift_ref, coef_ref, k, f).reshape(2, BLK, BLK)
    round_blocks(field_ref, slot_ref, rounded)
    apply_schur(schur_ref, rounded, slot_ref, by_slot, images, gap_ref)


def project_kernel(slot_ref, partial_ref, lift_ref, schur_ref, residual_ref, *rest):
    field_ref, images = rest[0], rest[1:6]
    coef_ref, rounded, by_slot = rest[6:]
    load_coefficients(partial_ref, coef_ref)
    for k in range(2):
        for f in range(6):
            lift = lifted(lift_ref, coef_ref, k, f).reshape(2, BLK, BLK)
            field_ref[k, 2 * f:2 * f + 2] = residual_ref[k, 2 * f:2 * f + 2] - lift
    round_blocks(field_ref, slot_ref, rounded)
    apply_schur(schur_ref, rounded, slot_ref, by_slot, images)


def step_kernel(slot_ref, partial_ref, lift_ref, schur_ref, image_ref, projected_ref, *rest):
    sums_ref, change_ref, field_ref, images = rest[0], rest[1], rest[2], rest[3:8]
    coef_ref, rounded, by_slot = rest[8:]
    sums = load_coefficients(partial_ref, coef_ref)[8:16]
    sums_ref[...] = sums
    alpha = sums[4:5] / sums[5:6]
    for k in range(2):
        for f in range(6):
            pair = slice(2 * f, 2 * f + 2)
            change = image_ref[k, pair] - lifted(lift_ref, coef_ref, k, f).reshape(2, BLK, BLK)
            change_ref[k, pair] = change
            field_ref[k, pair] = projected_ref[k, pair] - alpha[None] * change
    round_blocks(field_ref, slot_ref, rounded)
    apply_schur(schur_ref, rounded, slot_ref, by_slot, images)


def last_kernel(
    slot_ref, partial_ref, lift_ref, sums_ref, start_ref, first_ref, change_ref, second_ref, image_ref,
    multipliers_ref, norm_ref, coef_ref, by_slot,
):
    riders = load_coefficients(partial_ref, coef_ref)
    start_norm, start_curve = sums_ref[4:5], sums_ref[5:6]
    norm, second_curve, cross, back = riders[12:13], riders[13:14], riders[14:15], riders[15:16]
    alpha = start_norm / start_curve
    beta = norm / start_norm
    curve = second_curve + beta * (cross + back) + beta * beta * start_curve
    step = norm / curve
    total = jnp.zeros((1, BLK), F32)
    for k in range(2):
        for f in range(6):
            pair = slice(2 * f, 2 * f + 2)
            lift = lifted(lift_ref, coef_ref, k, f).reshape(2, BLK, BLK)
            change = (image_ref[k, pair] - lift) + beta[None] * change_ref[k, pair]
            second = second_ref[k, pair]
            left = second - step[None] * change
            total = total + jnp.sum((left * left).reshape(2 * BLK, BLK), axis=0, keepdims=True)
            first = first_ref[k, pair]
            direction = second + beta[None] * first
            by_slot[pair] = (start_ref[k, pair] + alpha[None] * first) + step[None] * direction
        for b in range(SLOTS):
            multipliers_ref[k, b * BLK:(b + 1) * BLK] = by_slot[slot_ref[k, b]]
    norm_ref[...] = jnp.broadcast_to(total[None], norm_ref.shape)


def combine_kernel(dots, swap_ref, length_ref, split_ref, *rest):
    parts, arrived = rest[0:5], rest[5:9]
    extras, (field_ref, terms_ref, line_ref) = rest[9:-3], rest[-3:]
    row = lax.broadcasted_iota(jnp.int32, (BLK, BLK), 0)
    line_ref[...] = jnp.zeros_like(line_ref)
    totals = [jnp.zeros((8, BLK), F32) for _ in dots]
    for k in range(2):
        for f in range(6):
            for c in range(2):
                q = 2 * f + c
                gap = own(parts, k, f, c) - partner(parts, arrived, swap_ref, k, f, c)
                block = jnp.where(row < length_ref[k, q], gap, 0.0)
                field_ref[k, q] = block
                for n, (left, right) in enumerate(dots):
                    a = block if left is None else extras[left][k, q]
                    b = block if right is None else extras[right][k, q]
                    totals[n] = totals[n] + jnp.sum((a * b).reshape(BLK // 8, 8, BLK), axis=0)
        pieces = thirds(field_ref[k].reshape(SLOTS * BLK, BLK))
        one = jnp.dot(split_ref[k], pieces[0], preferred_element_type=F32)
        two = jnp.dot(split_ref[k], pieces[1], preferred_element_type=F32)
        three = jnp.dot(split_ref[k], pieces[2], preferred_element_type=F32)
        terms = one[0:8] + ((one[8:16] + two[0:8]) + ((one[16:24] + two[8:16]) + three[0:8]))
        line_ref[MODES * k:MODES * (k + 1)] = terms[0:MODES]
    for n, total in enumerate(totals):
        line_ref[12 + n:13 + n] = jnp.sum(total, axis=0, keepdims=True)
    terms_ref[...] = jnp.broadcast_to(line_ref[...][None], terms_ref.shape)


def send(parts):
    def moved(value, axis, step):
        count = lax.axis_size(axis)
        return lax.ppermute(value, axis, [(i, (i + step) % count) for i in range(count)])

    sub = ("p", "core")
    return (
        moved(parts[2], "x", 1), moved(parts[1], "x", -1),
        moved(parts[4], sub, 1), moved(parts[3], sub, -1),
    )


def combine(dots, places, swaps, lengths, split, parts, *extras):
    kernel = functools.partial(combine_kernel, dots)
    out = (FIELD, shape(places, ROWS, BLK))
    specs = [SMEM] * 2 + [VMEM] * (10 + len(extras))
    return call(kernel, out, specs, [pltpu.VMEM((ROWS, BLK), F32)])(
        swaps, lengths, split, *parts, *send(parts), *extras
    )


def body(schur, local_gap, modes, rigid_loads, coarse_inverse, slots, swaps, lengths):
    places = lax.axis_size("p")
    core = jnp.full((1,), lax.axis_index("core"), jnp.int32)
    operator_flops = 2 * 2 * SLOTS * BLK * SLOTS * BLK * BLK
    operator_bytes = 2 * SLOTS * BLK * SLOTS * BLK * 2

    split, payload, *mode_parts = pack(slots, modes, rigid_loads, coarse_inverse, places)
    table, lift, *shares = unpack(core, swaps, lengths, payload, mode_parts)
    partial = collect(*shares)
    start, *images = call(
        first_kernel, (FIELD,) + PARTS, [SMEM] + [VMEM] * 4, SCRATCH, operator_flops, operator_bytes
    )(slots, partial, lift, schur, local_gap)
    residual, terms = combine((), places, swaps, lengths, split, images)

    partial = coarse_solve(core, table, terms)
    projected, *images = call(
        project_kernel, (FIELD,) + PARTS, [SMEM] + [VMEM] * 4, SCRATCH, operator_flops, operator_bytes
    )(slots, partial, lift, schur, residual)
    image, terms = combine(((0, 0), (0, None)), places, swaps, lengths, split, images, projected)

    partial = coarse_solve(core, table, terms)
    sums, change, second, *images = call(
        step_kernel, (shape(8, BLK), FIELD, FIELD) + PARTS, [SMEM] + [VMEM] * 5,
        SCRATCH, operator_flops, operator_bytes,
    )(slots, partial, lift, schur, image, projected)
    dots = ((0, 0), (0, None), (1, None), (0, 2))
    second_image, terms = combine(dots, places, swaps, lengths, split, images, second, projected, image)

    partial = coarse_solve(core, table, terms)
    multipliers, norm = call(
        last_kernel, (shape(2, SLOTS * BLK, BLK), shape(places, 8, BLK)), [SMEM] + [VMEM] * 8,
        [SCRATCH[0], SCRATCH[2]],
    )(slots, partial, lift, sums, start, projected, change, second, second_image)
    norm = jnp.sum(lax.all_to_all(norm, "p", 0, 0, tiled=True), axis=0)
    norm = norm + lax.ppermute(norm, "core", [(0, 1), (1, 0)])
    norm = lax.all_to_all(jnp.broadcast_to(norm[None], (4, 8, BLK)), "x", 0, 0, tiled=True)
    return multipliers, jnp.sqrt(jnp.sum(norm[:, 0], axis=0) / sums[4])


def solution(mesh):
    fine = Mesh(mesh.devices.reshape(-1, 2, 4), ("p", "core", "x"))
    everywhere = ("p", "core", "x")
    deep, flat = P(everywhere, None, None), P(everywhere, None)
    in_specs = (deep, deep, deep, deep, flat, flat, flat, flat)
    return jax.shard_map(body, mesh=fine, in_specs=in_specs, out_specs=(deep, P()), check_vma=False)
```

time: 244 us -> 209 us (0.86)
  Pallas kernels: 47 us -> 23.4 us
  blocking collectives: 113 us -> 94.7 us
  starting transfers between devices: 45.6 us -> 52.2 us
  local copies, waits for them, and re-layouts: 2.7 us -> 9.14 us
  waiting for transfers between devices: 31.1 us -> 26.9 us
  matrix products: 2.78 us -> 0 us
    all_to_all x4 -> x5, blocking collectives: 54.1 us -> 39.2 us  [the longest x4 32.6 us: collect(): return lax.all_to_all(both, 'x', 0, 0, tiled=True)]
    ppermute x2 -> x5, starting transfers between devices: 4.72 us -> 19 us  [the longest x4 15.6 us: collect(): both = mine + lax.ppermute(other, 'core', [(0, 1), (1, 0)])]
    all_to_all x3 -> x1, starting transfers between devices: 22 us -> 12.2 us  [unpack(): payload = lax.all_to_all(payload, 'p', 0, 0, tiled=True)]
    pallas_call x7, Pallas kernels: 21.7 us -> 12.1 us  [the longest x1 3.74 us: body(): call(first_kernel, (FIELD,) + PARTS, [SMEM] + [VMEM] * 4, SCRATCH, operat...]
    unnamed x15 -> x26, local copies, waits for them, and re-layouts: 0.17 us -> 9.14 us
    all_to_all x3 -> x1, waiting for transfers between devices: 6.59 us -> 0.28 us  [unpack(): payload = lax.all_to_all(payload, 'p', 0, 0, tiled=True)]
    ppermute x16, waiting for transfers between devices: 15.6 us -> 21.9 us  [moved(): lax.ppermute(value, axis, [(i, (i + step) % count) for i in range(count)])]
    pallas_call x1, Pallas kernels: 9.87 us -> 3.65 us  [body(): call(step_kernel, (shape(8, BLK), FIELD, FIELD) + PARTS, [SMEM] + [VMEM]...]
  transfers between devices with their start and end apart: 21 -> 22, of which waited for: 12 -> 17; matrix products, arithmetic and copies ran while one was open for 0% -> 0% of each run, Pallas kernels for 0% -> 0%
where the time goes in v2:
time: 209 us; the launch traced here: 208 us
  blocking collectives  94.7 us (45%)
  starting transfers between devices  52.2 us (25%)
  waiting for transfers between devices  26.9 us (13%)
  Pallas kernels  23.4 us (11%)
  local copies, waits for them, and re-layouts  9.14 us (4%)
    all_to_all x3, blocking collectives, coarse_solve(): gathered = lax.all_to_all(terms, 'p', 0, 0, tiled=True)  42.4 us
    all_to_all x4, blocking collectives, collect(): return lax.all_to_all(both, 'x', 0, 0, tiled=True)  32.6 us
    ppermute x16, waiting for transfers between devices, moved(): lax.ppermute(value, axis, [(i, (i + step) % count) for i in range(count)])  21.9 us
    ppermute x16, starting transfers between devices, moved(): lax.ppermute(value, axis, [(i, (i + step) % count) for i in range(count)])  21 us
    ppermute x4, starting transfers between devices, collect(): both = mine + lax.ppermute(other, 'core', [(0, 1), (1, 0)])  15.6 us
    all_to_all x1, blocking collectives, body(): norm = jnp.sum(lax.all_to_all(norm, 'p', 0, 0, tiled=True), axis=0)  13.2 us
    all_to_all x1, starting transfers between devices, unpack(): payload = lax.all_to_all(payload, 'p', 0, 0, tiled=True)  12.2 us
    unnamed x26, local copies, waits for them, and re-layouts  9.14 us
  transfers between devices with their start and end apart: 22, of which 17 were waited for; matrix products, arithmetic and copies ran while one was open for 0% of the time, Pallas kernels for 0%

profile of v2, /device:TPU:1, one launch (start us, length us, event | category | flops | bytes accessed | tf_op | source)
XLA Modules:
  0.0 207.8 jit_solution(11516212303083690300)
XLA Ops:
  0.7 1.0 copy-done.3
  3.9 1.9 shard_map.95
  6.7 12.2 %all-to-all-start = ((f32[32,32,128]{2,1,0:T(8,128)}), f32[32,32,128]{2,1,0:T(8,128)S(1)}, u32[]{:S(2)}, u32[]{:S(2)}) async-start(f32[32,32,128]{2,1,0:T(8,128)} %copy-done.2), calls=%async_computation | async-start | bytes 1048576 | tf_op jit(solution)/shard_map/all_to_all | solution.py:157
  18.9 2.6 %collective-permute-start.1 = (f32[2,2,8,128]{3,2,1,0:T(8,128)S(1)}, f32[2,2,8,128]{3,2,1,0:T(8,128)S(1)}, u32[]{:S(2)}, u32[]{:S(2)}) collective-permute-start(f32[2,2,8,128]{3,2,1,0:T(8,128)S(1)} %get-tuple-element.49.rest_1_), channel_id=1, source_target_pairs={{0,3},{1,0},{2,1},{3,2},{4,7},{5,4},{6,5},{7,6},{8,11},{9,8},{10,9... | collective-permute-start | bytes 49160 | tf_op jit(solution)/shard_map/ppermute | solution.py:322
  21.4 1.2 collective-permute-start.3
  22.7 1.4 collective-permute-start.2
  24.1 1.2 collective-permute-done.rest_5_
  25.2 7.7 %collective-permute-done.3.rest_8_ = f32[2,2,8,128]{3,2,1,0:T(8,128)S(1)} collective-permute-done((f32[2,2,8,128]{3,2,1,0:T(8,128)S(1)}, f32[2,2,8,128]{3,2,1,0:T(8,128)S(1)}, u32[]{:S(2)}, u32[]{:S(2)}) %collective-permute-start.3) | collective-permute-done | bytes 16416 | tf_op jit(solution)/shard_map/ppermute | solution.py:322
  34.5 1.3 shard_map.96
  35.8 4.3 %collective-permute-start.4 = (f32[4,64,128]{2,1,0:T(8,128)S(1)}, f32[4,64,128]{2,1,0:T(8,128)S(1)}, u32[]{:S(2)}, u32[]{:S(2)}) collective-permute-start(f32[4,64,128]{2,1,0:T(8,128)S(1)} %get-tuple-element.56), channel_id=1, source_target_pairs={{0,4},{4,0},{1,5},{5,1},{2,6},{6,2},{3,7},{7,3},{8,12},{12,8},{9,1... | collective-permute-start | bytes 393224 | tf_op jit(solution)/shard_map/ppermute | solution.py:167
  40.1 1.0 collective-permute-done.4
  41.1 8.6 %all_to_all.50.partial_ref = f32[4,64,128]{2,1,0:T(8,128)S(1)} all-to-all(f32[4,64,128]{2,1,0:T(8,128)S(1)} %add.15), channel_id=1, replica_groups=mesh['p'=32,'core'=2,'x'=4] {'x'}, dimensions={0} | all-to-all | bytes 262144 | tf_op jit(solution)/shard_map/all_to_all | solution.py:168
  49.7 3.7 %copy-done = bf16[2,1536,1536]{2,1,0:T(8,128)(2,1)S(1)} copy-done((bf16[2,1536,1536]{2,1,0:T(8,128)(2,1)S(1)}, bf16[2,1536,1536]{2,1,0:T(8,128)(2,1)}, u32[]{:S(2)}) %copy-start) | copy-done | bytes 9437208
  53.4 3.7 %shard_map.97 = (f32[2,12,128,128]{3,2,1,0:T(8,128)S(1)}, f32[2,4,128,128]{3,2,1,0:T(8,128)S(1)}, f32[2,2,128,128]{3,2,1,0:T(8,128)S(1)}, f32[2,2,128,128]{3,2,1...) custom-call(s32[2,12]{1,0:T(2,128)S(1)} %copy-done.6, ...), custom_call_target="tpu_custom_call" | custom-call | flops 1207959552 | bytes 9437184 | tf_op jit(solution)/shard_map/pallas_call | solution.py:349
  58.7 2.4 %collective-permute-start.8 = (f32[2,2,128,128]{3,2,1,0:T(8,128)S(1)}, f32[2,2,128,128]{3,2,1,0:T(8,128)S(1)}, u32[]{:S(2)}, u32[]{:S(2)}) collective-permute-start(f32[2,2,128,128]{3,2,1,0:T(8,128)S(1)} %get-tuple-element.61.rest_3_), channel_id=1, source_target_pairs={{0,252},{4,0},{8,4},{12,8},{16,12},{20,16},{24,20},{28,24},{32,28}... | collective-permute-start | bytes 786440 | tf_op jit(solution)/shard_map/ppermute | solution.py:322
  61.0 1.5 collective-permute-start.7
  63.2 1.8 collective-permute-done.5.rest_5_
  65.0 1.8 collective-permute-done.8.rest_8_
  66.9 1.4 shard_map.98
  68.3 14.0 %all_to_all.51.terms_ref = f32[32,16,128]{2,1,0:T(8,128)S(1)} all-to-all(f32[32,16,128]{2,1,0:T(8,128)S(1)} %get-tuple-element.63), channel_id=1, replica_groups=mesh['p'=32,'core'=2,'x'=4] {'p'}, dimensions={0} | all-to-all | bytes 524288 | tf_op jit(solution)/shard_map/all_to_all | solution.py:172
  82.9 3.9 %collective-permute-start.9 = (f32[4,64,128]{2,1,0:T(8,128)S(1)}, f32[4,64,128]{2,1,0:T(8,128)S(1)}, u32[]{:S(2)}, u32[]{:S(2)}) collective-permute-start(f32[4,64,128]{2,1,0:T(8,128)S(1)} %get-tuple-element.65), channel_id=1, source_target_pairs={{0,4},{4,0},{1,5},{5,1},{2,6},{6,2},{3,7},{7,3},{8,12},{12,8},{9,1... | collective-permute-start | bytes 393224 | tf_op jit(solution)/shard_map/ppermute | solution.py:167
  86.8 1.0 collective-permute-done.9
  87.8 8.0 %all_to_all.52.partial_ref = f32[4,64,128]{2,1,0:T(8,128)S(1)} all-to-all(f32[4,64,128]{2,1,0:T(8,128)S(1)} %add.16), channel_id=1, replica_groups=mesh['p'=32,'core'=2,'x'=4] {'x'}, dimensions={0} | all-to-all | bytes 262144 | tf_op jit(solution)/shard_map/all_to_all | solution.py:168
  95.8 3.6 %shard_map.100 = (f32[2,12,128,128]{3,2,1,0:T(8,128)S(1)}, f32[2,4,128,128]{3,2,1,0:T(8,128)S(1)}, f32[2,2,128,128]{3,2,1,0:T(8,128)S(1)}, f32[2,2,128,128]{3,2,...) custom-call(s32[2,12]{1,0:T(2,128)S(1)} %copy-done.6, ...), custom_call_target="tpu_custom_call" | custom-call | flops 1207959552 | bytes 9437184 | tf_op jit(solution)/shard_map/pallas_call | solution.py:355
  99.5 1.0 collective-permute-start.11
  101.0 2.4 %collective-permute-start.13 = (f32[2,2,128,128]{3,2,1,0:T(8,128)S(1)}, f32[2,2,128,128]{3,2,1,0:T(8,128)S(1)}, u32[]{:S(2)}, u32[]{:S(2)}) collective-permute-start(f32[2,2,128,128]{3,2,1,0:T(8,128)S(1)} %get-tuple-element.70.rest_3_), channel_id=1, source_target_pairs={{0,252},{4,0},{8,4},{12,8},{16,12},{20,16},{24,20},{28,24},{32,28}... | collective-permute-start | bytes 786440 | tf_op jit(solution)/shard_map/ppermute | solution.py:322
  103.4 1.3 collective-permute-start.12
  105.6 1.8 collective-permute-done.10.rest_5_
  107.4 1.7 collective-permute-done.13.rest_8_
  109.0 1.6 shard_map.101
  110.7 14.2 %all_to_all.53.terms_ref = f32[32,16,128]{2,1,0:T(8,128)S(1)} all-to-all(f32[32,16,128]{2,1,0:T(8,128)S(1)} %get-tuple-element.73), channel_id=1, replica_groups=mesh['p'=32,'core'=2,'x'=4] {'p'}, dimensions={0} | all-to-all | bytes 524288 | tf_op jit(solution)/shard_map/all_to_all | solution.py:172
  125.4 3.7 %collective-permute-start.14 = (f32[4,64,128]{2,1,0:T(8,128)S(1)}, f32[4,64,128]{2,1,0:T(8,128)S(1)}, u32[]{:S(2)}, u32[]{:S(2)}) collective-permute-start(f32[4,64,128]{2,1,0:T(8,128)S(1)} %get-tuple-element.75), channel_id=1, source_target_pairs={{0,4},{4,0},{1,5},{5,1},{2,6},{6,2},{3,7},{7,3},{8,12},{12,8},{9,1... | collective-permute-start | bytes 393224 | tf_op jit(solution)/shard_map/ppermute | solution.py:167
  129.1 1.0 collective-permute-done.14
  130.1 8.0 %all_to_all.54.partial_ref = f32[4,64,128]{2,1,0:T(8,128)S(1)} all-to-all(f32[4,64,128]{2,1,0:T(8,128)S(1)} %add.17), channel_id=1, replica_groups=mesh['p'=32,'core'=2,'x'=4] {'x'}, dimensions={0} | all-to-all | bytes 262144 | tf_op jit(solution)/shard_map/all_to_all | solution.py:168
  138.1 3.7 %shard_map.103 = (f32[8,128]{1,0:T(8,128)S(1)}, f32[2,12,128,128]{3,2,1,0:T(8,128)S(1)}, f32[2,12,128,128]{3,2,1,0:T(8,128)S(1)}, f32[2,4,128,128]{3,2,1,0:T(8,1...) custom-call(s32[2,12]{1,0:T(2,128)S(1)} %copy-done.6, ...), custom_call_target="tpu_custom_call" | custom-call | flops 1207959552 | bytes 9437184 | tf_op jit(solution)/shard_map/pallas_call | solution.py:361
  143.3 2.4 %collective-permute-start.18 = (f32[2,2,128,128]{3,2,1,0:T(8,128)S(1)}, f32[2,2,128,128]{3,2,1,0:T(8,128)S(1)}, u32[]{:S(2)}, u32[]{:S(2)}) collective-permute-start(f32[2,2,128,128]{3,2,1,0:T(8,128)S(1)} %get-tuple-element.80.rest_3_), channel_id=1, source_target_pairs={{0,252},{4,0},{8,4},{12,8},{16,12},{20,16},{24,20},{28,24},{32,28}... | collective-permute-start | bytes 786440 | tf_op jit(solution)/shard_map/ppermute | solution.py:322
  145.7 1.3 collective-permute-start.17
  147.9 1.8 collective-permute-done.15.rest_5_
  149.7 1.7 collective-permute-done.18.rest_8_
  151.4 1.9 shard_map.104
  153.2 14.2 %all_to_all.55.terms_ref = f32[32,16,128]{2,1,0:T(8,128)S(1)} all-to-all(f32[32,16,128]{2,1,0:T(8,128)S(1)} %get-tuple-element.83), channel_id=1, replica_groups=mesh['p'=32,'core'=2,'x'=4] {'p'}, dimensions={0} | all-to-all | bytes 524288 | tf_op jit(solution)/shard_map/all_to_all | solution.py:172
  167.9 3.7 %collective-permute-start.19 = (f32[4,64,128]{2,1,0:T(8,128)S(1)}, f32[4,64,128]{2,1,0:T(8,128)S(1)}, u32[]{:S(2)}, u32[]{:S(2)}) collective-permute-start(f32[4,64,128]{2,1,0:T(8,128)S(1)} %get-tuple-element.85), channel_id=1, source_target_pairs={{0,4},{4,0},{1,5},{5,1},{2,6},{6,2},{3,7},{7,3},{8,12},{12,8},{9,1... | collective-permute-start | bytes 393224 | tf_op jit(solution)/shard_map/ppermute | solution.py:167
  171.6 1.0 collective-permute-done.19
  172.7 8.0 %all_to_all.56.partial_ref = f32[4,64,128]{2,1,0:T(8,128)S(1)} all-to-all(f32[4,64,128]{2,1,0:T(8,128)S(1)} %add.18), channel_id=1, replica_groups=mesh['p'=32,'core'=2,'x'=4] {'x'}, dimensions={0} | all-to-all | bytes 262144 | tf_op jit(solution)/shard_map/all_to_all | solution.py:168
  180.6 2.7 %shard_map.106 = (f32[2,1536,128]{2,1,0:T(8,128)}, f32[32,8,128]{2,1,0:T(8,128)S(1)}) custom-call(s32[2,12]{1,0:T(2,128)S(1)} %copy-done.6, f32[4,64,128]{2,1,0:T(8,128)S(1)} %all_to_all.56.partial_ref, bf16[2,6,256,96]{3,2,1,0:T(8,128)(2,1)S(1)} %get-tuple-element.57.lift_ref, f32[8,128]{1,0:T(8,128)S(1)} %get-tuple-element.86.sums_ref, ...), custom_call_target="tpu_custom_call" | custom-call | tf_op jit(solution)/shard_map/pallas_call | solution.py:369
  183.3 13.2 %all_to_all.57 = f32[32,8,128]{2,1,0:T(8,128)S(1)} all-to-all(f32[32,8,128]{2,1,0:T(8,128)S(1)} %get-tuple-element.91), channel_id=1, replica_groups=mesh['p'=32,'core'=2,'x'=4] {'p'}, dimensions={0} | all-to-all | bytes 262144 | tf_op jit(solution)/shard_map/all_to_all | solution.py:373
  196.5 3.4 %collective-permute-start.20 = (f32[8,128]{1,0:T(8,128)S(1)}, f32[8,128]{1,0:T(8,128)S(1)}, u32[]{:S(2)}, u32[]{:S(2)}) collective-permute-start(f32[8,128]{1,0:T(8,128)S(1)} %reduce_sum.18), channel_id=1, source_target_pairs={{0,4},{4,0},{1,5},{5,1},{2,6},{6,2},{3,7},{7,3},{8,12},{12,8},{9,1... | collective-permute-start | bytes 12296 | tf_op jit(solution)/shard_map/ppermute | solution.py:374
  200.7 6.5 %all_to_all.58 = f32[4,8,128]{2,1,0:T(8,128)S(1)} all-to-all(f32[4,8,128]{2,1,0:T(8,128)S(1)} %broadcast_in_dim.10), channel_id=1, replica_groups=mesh['p'=32,'core'=2,'x'=4] {'x'}, dimensions={0} | all-to-all | bytes 32768 | tf_op jit(solution)/shard_map/all_to_all | solution.py:375
  (54 shorter events, 13.8 us)
Async XLA Ops:
  0.6 49.1 %copy-start.1 = (f32[2,1536,128]{2,1,0:T(8,128)S(1)}, f32[2,1536,128]{2,1,0:T(8,128)}, u32[]{:S(2)}) copy-start(f32[2,1536,128]{2,1,0:T(8,128)} %gap_ref.1) | copy-start | bytes 4718596
  0.6 1.0 copy-start.3
  1.7 0.9 copy-start.4
  2.6 0.7 copy-start.5
  3.3 0.7 copy-start.9
  3.9 45.8 %copy-start.6 = (s32[2,12]{1,0:T(2,128)S(1)}, s32[2,12]{1,0:T(2,128)}, u32[]{:S(2)}) copy-start(s32[2,12]{1,0:T(2,128)} %slot_ref.9) | copy-start | bytes 292
  5.9 0.8 copy-start.2
  6.7 89.1 %slice-start = ((s8[9437184]{0:T(1024)(128)(4,1)}), s8[1048576]{0:T(1024)(128)(4,1)S(1)}, s32[]{:S(2)}) async-start(s8[9437184]{0:T(1024)(128)(4,1)} %bitcast.8), calls=%async_computation.10 | async-start | bytes 2097152
  6.7 26.5 %all-to-all-start = ((f32[32,32,128]{2,1,0:T(8,128)}), f32[32,32,128]{2,1,0:T(8,128)S(1)}, u32[]{:S(2)}, u32[]{:S(2)}) async-start(f32[32,32,128]{2,1,0:T(8,128)} %copy-done.2), calls=%async_computation | async-start | bytes 1048576 | tf_op jit(solution)/shard_map/all_to_all | solution.py:157
  18.9 5.2 %collective-permute-start.1 = (f32[2,2,8,128]{3,2,1,0:T(8,128)S(1)}, f32[2,2,8,128]{3,2,1,0:T(8,128)S(1)}, u32[]{:S(2)}, u32[]{:S(2)}) collective-permute-start(f32[2,2,8,128]{3,2,1,0:T(8,128)S(1)} %get-tuple-element.49.rest_1_), channel_id=1, source_target_pairs={{0,3},{1,0},{2,1},{3,2},{4,7},{5,4},{6,5},{7,6},{8,11},{9,8},{10,9... | collective-permute-start | bytes 49160 | tf_op jit(solution)/shard_map/ppermute | solution.py:322
  21.4 3.8 %collective-permute-start = (f32[2,2,8,128]{3,2,1,0:T(8,128)S(1)}, f32[2,2,8,128]{3,2,1,0:T(8,128)S(1)}, u32[]{:S(2)}, u32[]{:S(2)}) collective-permute-start(f32[2,2,8,128]{3,2,1,0:T(8,128)S(1)} %get-tuple-element.50.rest_2_), channel_id=1, source_target_pairs={{0,1},{1,2},{2,3},{3,0},{4,5},{5,6},{6,7},{7,4},{8,9},{9,10},{10,1... | collective-permute-start | bytes 49160 | tf_op jit(solution)/shard_map/ppermute | solution.py:322
  21.4 11.5 %collective-permute-start.3 = (f32[2,2,8,128]{3,2,1,0:T(8,128)S(1)}, f32[2,2,8,128]{3,2,1,0:T(8,128)S(1)}, u32[]{:S(2)}, u32[]{:S(2)}) collective-permute-start(f32[2,2,8,128]{3,2,1,0:T(8,128)S(1)} %get-tuple-element.51.rest_3_), channel_id=1, source_target_pairs={{0,252},{4,0},{8,4},{12,8},{16,12},{20,16},{24,20},{28,24},{32,28}... | collective-permute-start | bytes 49160 | tf_op jit(solution)/shard_map/ppermute | solution.py:322
  22.7 10.2 %collective-permute-start.2 = (f32[2,2,8,128]{3,2,1,0:T(8,128)S(1)}, f32[2,2,8,128]{3,2,1,0:T(8,128)S(1)}, u32[]{:S(2)}, u32[]{:S(2)}) collective-permute-start(f32[2,2,8,128]{3,2,1,0:T(8,128)S(1)} %get-tuple-element.52.rest_4_), channel_id=1, source_target_pairs={{0,4},{4,8},{8,12},{12,16},{16,20},{20,24},{24,28},{28,32},{32,36}... | collective-permute-start | bytes 49160 | tf_op jit(solution)/shard_map/ppermute | solution.py:322
  33.2 0.7 copy-start.7
  33.9 0.7 copy-start.8
  35.8 5.2 %collective-permute-start.4 = (f32[4,64,128]{2,1,0:T(8,128)S(1)}, f32[4,64,128]{2,1,0:T(8,128)S(1)}, u32[]{:S(2)}, u32[]{:S(2)}) collective-permute-start(f32[4,64,128]{2,1,0:T(8,128)S(1)} %get-tuple-element.56), channel_id=1, source_target_pairs={{0,4},{4,0},{1,5},{5,1},{2,6},{6,2},{3,7},{7,3},{8,12},{12,8},{9,1... | collective-permute-start | bytes 393224 | tf_op jit(solution)/shard_map/ppermute | solution.py:167
  49.7 3.7 %copy-start = (bf16[2,1536,1536]{2,1,0:T(8,128)(2,1)S(1)}, bf16[2,1536,1536]{2,1,0:T(8,128)(2,1)}, u32[]{:S(2)}) copy-start(bf16[2,1536,1536]{2,1,0:T(8,128)(2,1)} %schur_ref.5) | copy-start | bytes 28311556
  53.4 42.4 %slice-start.1 = ((s8[9437184]{0:T(1024)(128)(4,1)}), s8[4194304]{0:T(1024)(128)(4,1)S(1)}, s32[]{:S(2)}) async-start(s8[9437184]{0:T(1024)(128)(4,1)} %bitcast.8), calls=%async_computation.11 | async-start | bytes 8388608
  53.4 42.4 %slice-start.2 = ((s8[9437184]{0:T(1024)(128)(4,1)}), s8[4194304]{0:T(1024)(128)(4,1)S(1)}, s32[]{:S(2)}) async-start(s8[9437184]{0:T(1024)(128)(4,1)} %bitcast.8), calls=%async_computation.12 | async-start | bytes 8388608
  57.1 6.1 %collective-permute-start.6 = (f32[2,2,128,128]{3,2,1,0:T(8,128)S(1)}, f32[2,2,128,128]{3,2,1,0:T(8,128)S(1)}, u32[]{:S(2)}, u32[]{:S(2)}) collective-permute-start(f32[2,2,128,128]{3,2,1,0:T(8,128)S(1)} %get-tuple-element.59.rest_1_), channel_id=1, source_target_pairs={{0,3},{1,0},{2,1},{3,2},{4,7},{5,4},{6,5},{7,6},{8,11},{9,8},{10,9... | collective-permute-start | bytes 786440 | tf_op jit(solution)/shard_map/ppermute | solution.py:322
  58.1 6.9 %collective-permute-start.5 = (f32[2,2,128,128]{3,2,1,0:T(8,128)S(1)}, f32[2,2,128,128]{3,2,1,0:T(8,128)S(1)}, u32[]{:S(2)}, u32[]{:S(2)}) collective-permute-start(f32[2,2,128,128]{3,2,1,0:T(8,128)S(1)} %get-tuple-element.60.rest_2_), channel_id=1, source_target_pairs={{0,1},{1,2},{2,3},{3,0},{4,5},{5,6},{6,7},{7,4},{8,9},{9,10},{10,1... | collective-permute-start | bytes 786440 | tf_op jit(solution)/shard_map/ppermute | solution.py:322
  58.7 8.2 %collective-permute-start.8 = (f32[2,2,128,128]{3,2,1,0:T(8,128)S(1)}, f32[2,2,128,128]{3,2,1,0:T(8,128)S(1)}, u32[]{:S(2)}, u32[]{:S(2)}) collective-permute-start(f32[2,2,128,128]{3,2,1,0:T(8,128)S(1)} %get-tuple-element.61.rest_3_), channel_id=1, source_target_pairs={{0,252},{4,0},{8,4},{12,8},{16,12},{20,16},{24,20},{28,24},{32,28}... | collective-permute-start | bytes 786440 | tf_op jit(solution)/shard_map/ppermute | solution.py:322
  61.0 5.8 %collective-permute-start.7 = (f32[2,2,128,128]{3,2,1,0:T(8,128)S(1)}, f32[2,2,128,128]{3,2,1,0:T(8,128)S(1)}, u32[]{:S(2)}, u32[]{:S(2)}) collective-permute-start(f32[2,2,128,128]{3,2,1,0:T(8,128)S(1)} %get-tuple-element.62.rest_4_), channel_id=1, source_target_pairs={{0,4},{4,8},{8,12},{12,16},{16,20},{20,24},{24,28},{28,32},{32,36}... | collective-permute-start | bytes 786440 | tf_op jit(solution)/shard_map/ppermute | solution.py:322
  82.9 4.9 %collective-permute-start.9 = (f32[4,64,128]{2,1,0:T(8,128)S(1)}, f32[4,64,128]{2,1,0:T(8,128)S(1)}, u32[]{:S(2)}, u32[]{:S(2)}) collective-permute-start(f32[4,64,128]{2,1,0:T(8,128)S(1)} %get-tuple-element.65), channel_id=1, source_target_pairs={{0,4},{4,0},{1,5},{5,1},{2,6},{6,2},{3,7},{7,3},{8,12},{12,8},{9,1... | collective-permute-start | bytes 393224 | tf_op jit(solution)/shard_map/ppermute | solution.py:167
  99.5 6.1 %collective-permute-start.11 = (f32[2,2,128,128]{3,2,1,0:T(8,128)S(1)}, f32[2,2,128,128]{3,2,1,0:T(8,128)S(1)}, u32[]{:S(2)}, u32[]{:S(2)}) collective-permute-start(f32[2,2,128,128]{3,2,1,0:T(8,128)S(1)} %get-tuple-element.68.rest_1_), channel_id=1, source_target_pairs={{0,3},{1,0},{2,1},{3,2},{4,7},{5,4},{6,5},{7,6},{8,11},{9,8},{10,9... | collective-permute-start | bytes 786440 | tf_op jit(solution)/shard_map/ppermute | solution.py:322
  100.4 6.9 %collective-permute-start.10 = (f32[2,2,128,128]{3,2,1,0:T(8,128)S(1)}, f32[2,2,128,128]{3,2,1,0:T(8,128)S(1)}, u32[]{:S(2)}, u32[]{:S(2)}) collective-permute-start(f32[2,2,128,128]{3,2,1,0:T(8,128)S(1)} %get-tuple-element.69.rest_2_), channel_id=1, source_target_pairs={{0,1},{1,2},{2,3},{3,0},{4,5},{5,6},{6,7},{7,4},{8,9},{9,10},{10,1... | collective-permute-start | bytes 786440 | tf_op jit(solution)/shard_map/ppermute | solution.py:322
  101.0 8.0 %collective-permute-start.13 = (f32[2,2,128,128]{3,2,1,0:T(8,128)S(1)}, f32[2,2,128,128]{3,2,1,0:T(8,128)S(1)}, u32[]{:S(2)}, u32[]{:S(2)}) collective-permute-start(f32[2,2,128,128]{3,2,1,0:T(8,128)S(1)} %get-tuple-element.70.rest_3_), channel_id=1, source_target_pairs={{0,252},{4,0},{8,4},{12,8},{16,12},{20,16},{24,20},{28,24},{32,28}... | collective-permute-start | bytes 786440 | tf_op jit(solution)/shard_map/ppermute | solution.py:322
  103.4 5.7 %collective-permute-start.12 = (f32[2,2,128,128]{3,2,1,0:T(8,128)S(1)}, f32[2,2,128,128]{3,2,1,0:T(8,128)S(1)}, u32[]{:S(2)}, u32[]{:S(2)}) collective-permute-start(f32[2,2,128,128]{3,2,1,0:T(8,128)S(1)} %get-tuple-element.71.rest_4_), channel_id=1, source_target_pairs={{0,4},{4,8},{8,12},{12,16},{16,20},{20,24},{24,28},{28,32},{32,36}... | collective-permute-start | bytes 786440 | tf_op jit(solution)/shard_map/ppermute | solution.py:322
  125.4 4.7 %collective-permute-start.14 = (f32[4,64,128]{2,1,0:T(8,128)S(1)}, f32[4,64,128]{2,1,0:T(8,128)S(1)}, u32[]{:S(2)}, u32[]{:S(2)}) collective-permute-start(f32[4,64,128]{2,1,0:T(8,128)S(1)} %get-tuple-element.75), channel_id=1, source_target_pairs={{0,4},{4,0},{1,5},{5,1},{2,6},{6,2},{3,7},{7,3},{8,12},{12,8},{9,1... | collective-permute-start | bytes 393224 | tf_op jit(solution)/shard_map/ppermute | solution.py:167
  141.8 6.1 %collective-permute-start.16 = (f32[2,2,128,128]{3,2,1,0:T(8,128)S(1)}, f32[2,2,128,128]{3,2,1,0:T(8,128)S(1)}, u32[]{:S(2)}, u32[]{:S(2)}) collective-permute-start(f32[2,2,128,128]{3,2,1,0:T(8,128)S(1)} %get-tuple-element.78.rest_1_), channel_id=1, source_target_pairs={{0,3},{1,0},{2,1},{3,2},{4,7},{5,4},{6,5},{7,6},{8,11},{9,8},{10,9... | collective-permute-start | bytes 786440 | tf_op jit(solution)/shard_map/ppermute | solution.py:322
  142.7 6.9 %collective-permute-start.15 = (f32[2,2,128,128]{3,2,1,0:T(8,128)S(1)}, f32[2,2,128,128]{3,2,1,0:T(8,128)S(1)}, u32[]{:S(2)}, u32[]{:S(2)}) collective-permute-start(f32[2,2,128,128]{3,2,1,0:T(8,128)S(1)} %get-tuple-element.79.rest_2_), channel_id=1, source_target_pairs={{0,1},{1,2},{2,3},{3,0},{4,5},{5,6},{6,7},{7,4},{8,9},{9,10},{10,1... | collective-permute-start | bytes 786440 | tf_op jit(solution)/shard_map/ppermute | solution.py:322
  143.3 8.0 %collective-permute-start.18 = (f32[2,2,128,128]{3,2,1,0:T(8,128)S(1)}, f32[2,2,128,128]{3,2,1,0:T(8,128)S(1)}, u32[]{:S(2)}, u32[]{:S(2)}) collective-permute-start(f32[2,2,128,128]{3,2,1,0:T(8,128)S(1)} %get-tuple-element.80.rest_3_), channel_id=1, source_target_pairs={{0,252},{4,0},{8,4},{12,8},{16,12},{20,16},{24,20},{28,24},{32,28}... | collective-permute-start | bytes 786440 | tf_op jit(solution)/shard_map/ppermute | solution.py:322
  145.7 5.7 %collective-permute-start.17 = (f32[2,2,128,128]{3,2,1,0:T(8,128)S(1)}, f32[2,2,128,128]{3,2,1,0:T(8,128)S(1)}, u32[]{:S(2)}, u32[]{:S(2)}) collective-permute-start(f32[2,2,128,128]{3,2,1,0:T(8,128)S(1)} %get-tuple-element.81.rest_4_), channel_id=1, source_target_pairs={{0,4},{4,8},{8,12},{12,16},{16,20},{20,24},{24,28},{28,32},{32,36}... | collective-permute-start | bytes 786440 | tf_op jit(solution)/shard_map/ppermute | solution.py:322
  167.9 4.7 %collective-permute-start.19 = (f32[4,64,128]{2,1,0:T(8,128)S(1)}, f32[4,64,128]{2,1,0:T(8,128)S(1)}, u32[]{:S(2)}, u32[]{:S(2)}) collective-permute-start(f32[4,64,128]{2,1,0:T(8,128)S(1)} %get-tuple-element.85), channel_id=1, source_target_pairs={{0,4},{4,0},{1,5},{5,1},{2,6},{6,2},{3,7},{7,3},{8,12},{12,8},{9,1... | collective-permute-start | bytes 393224 | tf_op jit(solution)/shard_map/ppermute | solution.py:167
  196.5 4.2 %collective-permute-start.20 = (f32[8,128]{1,0:T(8,128)S(1)}, f32[8,128]{1,0:T(8,128)S(1)}, u32[]{:S(2)}, u32[]{:S(2)}) collective-permute-start(f32[8,128]{1,0:T(8,128)S(1)} %reduce_sum.18), channel_id=1, source_target_pairs={{0,4},{4,0},{1,5},{5,1},{2,6},{6,2},{3,7},{7,3},{8,12},{12,8},{9,1... | collective-permute-start | bytes 12296 | tf_op jit(solution)/shard_map/ppermute | solution.py:374

commit v3 on v2

--- a/solution.py
+++ b/solution.py
@@ -11,26 +11,29 @@
 SLOTS = 12
 MODES = 6
 ROWS = 16
+PACK_ROOM = 60
+NORM_ROWS = 1
 SPLIT_LEFT = (0, 0, 1, 0, 1, 2)
 SPLIT_RIGHT = (0, 1, 0, 2, 1, 0)
 F32 = jnp.float32
 BF16 = jnp.bfloat16
 VMEM = pl.BlockSpec(memory_space=pltpu.VMEM)
 SMEM = pl.BlockSpec(memory_space=pltpu.SMEM)
+ANY = pl.BlockSpec(memory_space=pl.ANY)
 
 
 def shape(*dims, kind=F32):
     return jax.ShapeDtypeStruct(dims, kind)
 
 
-def call(kernel, out, in_specs, scratch=(), flops=0, moved=0):
+def call(kernel, out, in_specs, scratch=(), flops=0, moved=0, room=18):
     return pl.pallas_call(
         kernel,
         out_shape=out,
         in_specs=in_specs,
         out_specs=jax.tree.map(lambda _: VMEM, out),
         scratch_shapes=list(scratch),
-        compiler_params=pltpu.CompilerParams(vmem_limit_bytes=24 * 2**20),
+        compiler_params=pltpu.CompilerParams(vmem_limit_bytes=room * 2**20),
         cost_estimate=pl.CostEstimate(flops=flops, bytes_accessed=moved, transcendentals=0),
     )
 
@@ -44,15 +47,14 @@
 
 
 def pack_kernel(slot_ref, modes_ref, loads_ref, coarse_ref, split_ref, payload_ref, *rest):
-    parts, (by_slot, rows, line) = rest[:5], rest[5:]
+    by_slot, parts, (rows, line) = rest[0], rest[1:5], rest[5:]
     by_slot[...] = jnp.zeros_like(by_slot)
     for k in range(2):
         for b in range(SLOTS):
             for i in range(MODES):
                 by_slot[k, slot_ref[k, b], i:i + 1] = modes_ref[i, k:k + 1, b * BLK:(b + 1) * BLK]
-    parts[0][...] = by_slot[:, 0:4]
     for n in range(4):
-        parts[n + 1][...] = by_slot[:, 4 + 2 * n:6 + 2 * n]
+        parts[n][...] = by_slot[:, 4 + 2 * n:6 + 2 * n]
     rows[...] = jnp.zeros_like(rows)
     rows[0:12] = coarse_ref[...]
     line[...] = jnp.zeros_like(line)
@@ -80,15 +82,16 @@
 def pack(slots, modes, loads, coarse_inverse, places):
     return call(
         pack_kernel,
-        (shape(2, 32, SLOTS * BLK, kind=BF16), shape(places, 32, BLK), shape(2, 4, 8, BLK))
+        (shape(2, 32, SLOTS * BLK, kind=BF16), shape(places, 32, BLK), shape(2, SLOTS, 8, BLK))
         + (shape(2, 2, 8, BLK),) * 4,
         [SMEM] + [VMEM] * 3,
-        [pltpu.VMEM((2, SLOTS, 8, BLK), F32), pltpu.VMEM((ROWS, 96 * places), F32), pltpu.VMEM((ROWS, BLK), F32)],
+        [pltpu.VMEM((ROWS, 96 * places), F32), pltpu.VMEM((ROWS, BLK), F32)],
+        room=PACK_ROOM,
     )(slots, modes.transpose(1, 0, 2), loads.transpose(1, 0, 2), coarse_inverse)
 
 
-def partner(parts, arrived, swap_ref, k, f, c):
-    meets = jnp.bitwise_xor(swap_ref[k, f], c)
+def partner(parts, arrived, layout_ref, k, f, c):
+    meets = jnp.bitwise_xor(layout_ref[k, f], c)
     if f == 0:
         return parts[0][1 - k, 2 + meets]
     if f == 1:
@@ -115,14 +118,15 @@
             out_ref[x, 52:64] = solved[c + 2, x, 0:12]
 
 
-def partial_kernel(core_ref, table_ref, terms_ref, mine_ref, other_ref, solved):
+def partial_kernel(core_ref, table_ref, terms_ref, *rest):
+    mine_ref, other_ref, solved = rest[-3:]
     riders = jnp.sum(terms_ref[:, 8:16], axis=0)[4:8]
     share(core_ref[0], table_ref[...], terms_ref[...].reshape(-1, BLK), riders, mine_ref, other_ref, solved)
 
 
-def unpack_kernel(core_ref, swap_ref, length_ref, payload_ref, *rest):
-    parts, arrived = rest[0:5], rest[5:9]
-    table_ref, lift_ref, mine_ref, other_ref, wide, terms, solved = rest[9:]
+def unpack_kernel(core_ref, layout_ref, payload_ref, modes_ref, *rest):
+    arrived = rest[0:4]
+    table_ref, lift_ref, mine_ref, other_ref, wide, terms, solved = rest[-7:]
     places = payload_ref.shape[0]
     terms[...] = jnp.zeros_like(terms)
     wide[...] = jnp.zeros_like(wide)
@@ -139,9 +143,11 @@
     for k in range(2):
         for f in range(6):
             for c in range(2):
-                live = lane < length_ref[k, 2 * f + c]
-                mine = jnp.where(live, own(parts, k, f, c), 0.0)
-                theirs = jnp.where(live, -partner(parts, arrived, swap_ref, k, f, c), 0.0)
+                live = lane < layout_ref[k, 6 + 2 * f + c]
+                meets = jnp.bitwise_xor(layout_ref[k, f], c)
+                theirs = modes_ref[1 - k, 2 * (1 - f) + meets] if f < 2 else arrived[f - 2][k, meets]
+                mine = jnp.where(live, modes_ref[k, 2 * f + c], 0.0)
+                theirs = jnp.where(live, -theirs, 0.0)
                 both = jnp.concatenate([mine[0:MODES], theirs[0:MODES], mine[MODES:8], mine[MODES:8]], axis=0)
                 pieces = [piece.astype(F32) for piece in thirds(both)]
                 left = jnp.concatenate([pieces[n] for n in SPLIT_LEFT], axis=0)
@@ -152,15 +158,15 @@
 SOLVED = pltpu.VMEM((4, 4, ROWS, BLK), F32)
 
 
-def unpack(core, swaps, lengths, payload, parts):
+def unpack(core, layout, payload, modes, parts, *beside):
     places = payload.shape[0]
     payload = lax.all_to_all(payload, "p", 0, 0, tiled=True)
     return call(
         unpack_kernel,
         (shape(192, places * ROWS), shape(2, 6, 2 * BLK, 6 * ROWS, kind=BF16)) + SHARES,
-        [SMEM] * 3 + [VMEM] * 10,
+        [SMEM] * 2 + [VMEM] * (6 + len(beside)),
         [pltpu.VMEM((places * ROWS, 2 * BLK), F32), pltpu.VMEM((places * ROWS, BLK), F32), SOLVED],
-    )(core, swaps, lengths, payload, *parts, *send(parts))
+    )(core, layout, payload, modes, *send((None, *parts)), *beside)
 
 
 def collect(mine, other):
@@ -168,9 +174,10 @@
     return lax.all_to_all(both, "x", 0, 0, tiled=True)
 
 
-def coarse_solve(core, table, terms):
+def coarse_solve(core, table, terms, *beside):
     gathered = lax.all_to_all(terms, "p", 0, 0, tiled=True)
-    return collect(*call(partial_kernel, SHARES, [SMEM] + [VMEM] * 2, [SOLVED])(core, table, gathered))
+    specs = [SMEM] + [VMEM] * (2 + len(beside))
+    return collect(*call(partial_kernel, SHARES, specs, [SOLVED])(core, table, gathered, *beside))
 
 
 def load_coefficients(partial_ref, coef_ref):
@@ -214,6 +221,7 @@
 
 PARTS = (shape(2, 4, BLK, BLK),) + (shape(2, 2, BLK, BLK),) * 4
 FIELD = shape(2, SLOTS, BLK, BLK)
+MARK = shape(8, BLK)
 SCRATCH = [
     pltpu.VMEM((2, 6, ROWS, BLK), F32),
     pltpu.VMEM((2, SLOTS * BLK, BLK), BF16),
@@ -222,8 +230,8 @@
 
 
 def first_kernel(slot_ref, partial_ref, lift_ref, schur_ref, gap_ref, *rest):
-    field_ref, images = rest[0], rest[1:6]
-    coef_ref, rounded, by_slot = rest[6:]
+    images = rest[0:5]
+    coef_ref, rounded, by_slot, field_ref = rest[5:]
     load_coefficients(partial_ref, coef_ref)
     for k in range(2):
         for f in range(6):
@@ -261,34 +269,51 @@
 
 
 def last_kernel(
-    slot_ref, partial_ref, lift_ref, sums_ref, start_ref, first_ref, change_ref, second_ref, image_ref,
-    multipliers_ref, norm_ref, coef_ref, by_slot,
+    partial_ref, lift_ref, sums_ref, change_ref, second_ref, image_ref, norm_ref, scale_ref, coef_ref
 ):
     riders = load_coefficients(partial_ref, coef_ref)
     start_norm, start_curve = sums_ref[4:5], sums_ref[5:6]
     norm, second_curve, cross, back = riders[12:13], riders[13:14], riders[14:15], riders[15:16]
-    alpha = start_norm / start_curve
     beta = norm / start_norm
     curve = second_curve + beta * (cross + back) + beta * beta * start_curve
     step = norm / curve
-    total = jnp.zeros((1, BLK), F32)
+    scale_ref[...] = jnp.zeros_like(scale_ref)
+    scale_ref[0:1] = start_norm / start_curve
+    scale_ref[1:2] = beta
+    scale_ref[2:3] = step
+    total = jnp.zeros((8, BLK), F32)
     for k in range(2):
         for f in range(6):
             pair = slice(2 * f, 2 * f + 2)
             lift = lifted(lift_ref, coef_ref, k, f).reshape(2, BLK, BLK)
             change = (image_ref[k, pair] - lift) + beta[None] * change_ref[k, pair]
-            second = second_ref[k, pair]
-            left = second - step[None] * change
-            total = total + jnp.sum((left * left).reshape(2 * BLK, BLK), axis=0, keepdims=True)
+            left = second_ref[k, pair] - step[None] * change
+            total = total + jnp.sum((left * left).reshape(-1, 8, BLK), axis=0)
+    norm_ref[...] = jnp.broadcast_to(jnp.sum(total, axis=0, keepdims=True)[None], norm_ref.shape)
+
+
+def total_kernel(norm_ref, beside_ref, total_ref):
+    total_ref[...] = jnp.sum(norm_ref[...], axis=0)
+
+
+def multipliers_kernel(
+    slot_ref, scale_ref, partial_ref, lift_ref, first_ref, second_ref, multipliers_ref, mark_ref, coef_ref, by_slot
+):
+    load_coefficients(partial_ref, coef_ref)
+    alpha, beta, step = scale_ref[0:1], scale_ref[1:2], scale_ref[2:3]
+    for k in range(2):
+        for f in range(6):
+            pair = slice(2 * f, 2 * f + 2)
+            start = lifted(lift_ref, coef_ref, k, f).reshape(2, BLK, BLK)
             first = first_ref[k, pair]
-            direction = second + beta[None] * first
-            by_slot[pair] = (start_ref[k, pair] + alpha[None] * first) + step[None] * direction
+            direction = second_ref[k, pair] + beta[None] * first
+            by_slot[pair] = (start + alpha[None] * first) + step[None] * direction
         for b in range(SLOTS):
             multipliers_ref[k, b * BLK:(b + 1) * BLK] = by_slot[slot_ref[k, b]]
-    norm_ref[...] = jnp.broadcast_to(total[None], norm_ref.shape)
-
-
-def combine_kernel(dots, swap_ref, length_ref, split_ref, *rest):
+    mark_ref[...] = jnp.zeros_like(mark_ref)
+
+
+def combine_kernel(dots, layout_ref, split_ref, *rest):
     parts, arrived = rest[0:5], rest[5:9]
     extras, (field_ref, terms_ref, line_ref) = rest[9:-3], rest[-3:]
     row = lax.broadcasted_iota(jnp.int32, (BLK, BLK), 0)
@@ -298,8 +323,8 @@
         for f in range(6):
             for c in range(2):
                 q = 2 * f + c
-                gap = own(parts, k, f, c) - partner(parts, arrived, swap_ref, k, f, c)
-                block = jnp.where(row < length_ref[k, q], gap, 0.0)
+                gap = own(parts, k, f, c) - partner(parts, arrived, layout_ref, k, f, c)
+                block = jnp.where(row < layout_ref[k, 6 + q], gap, 0.0)
                 field_ref[k, q] = block
                 for n, (left, right) in enumerate(dots):
                     a = block if left is None else extras[left][k, q]
@@ -328,12 +353,12 @@
     )
 
 
-def combine(dots, places, swaps, lengths, split, parts, *extras):
+def combine(dots, places, layout, split, parts, *extras):
     kernel = functools.partial(combine_kernel, dots)
     out = (FIELD, shape(places, ROWS, BLK))
-    specs = [SMEM] * 2 + [VMEM] * (10 + len(extras))
+    specs = [SMEM] + [VMEM] * (10 + len(extras))
     return call(kernel, out, specs, [pltpu.VMEM((ROWS, BLK), F32)])(
-        swaps, lengths, split, *parts, *send(parts), *extras
+        layout, split, *parts, *send(parts), *extras
     )
 
 
@@ -343,36 +368,41 @@
     operator_flops = 2 * 2 * SLOTS * BLK * SLOTS * BLK * BLK
     operator_bytes = 2 * SLOTS * BLK * SLOTS * BLK * 2
 
-    split, payload, *mode_parts = pack(slots, modes, rigid_loads, coarse_inverse, places)
-    table, lift, *shares = unpack(core, swaps, lengths, payload, mode_parts)
-    partial = collect(*shares)
-    start, *images = call(
-        first_kernel, (FIELD,) + PARTS, [SMEM] + [VMEM] * 4, SCRATCH, operator_flops, operator_bytes
-    )(slots, partial, lift, schur, local_gap)
-    residual, terms = combine((), places, swaps, lengths, split, images)
-
-    partial = coarse_solve(core, table, terms)
+    layout = jnp.concatenate([swaps, lengths], axis=1)
+    split, payload, own_modes, *mode_parts = pack(slots, modes, rigid_loads, coarse_inverse, places)
+    table, lift, *shares = unpack(core, layout, payload, own_modes, mode_parts)
+    started = collect(*shares)
+    images = call(
+        first_kernel, PARTS, [SMEM] + [VMEM] * 4, SCRATCH + [pltpu.VMEM((2, SLOTS, BLK, BLK), F32)],
+        operator_flops, operator_bytes,
+    )(slots, started, lift, schur, local_gap)
+    residual, terms = combine((), places, layout, split, images)
+
+    partial = coarse_solve(core, table, terms, schur)
     projected, *images = call(
         project_kernel, (FIELD,) + PARTS, [SMEM] + [VMEM] * 4, SCRATCH, operator_flops, operator_bytes
     )(slots, partial, lift, schur, residual)
-    image, terms = combine(((0, 0), (0, None)), places, swaps, lengths, split, images, projected)
-
-    partial = coarse_solve(core, table, terms)
+    image, terms = combine(((0, 0), (0, None)), places, layout, split, images, projected)
+
+    partial = coarse_solve(core, table, terms, schur)
     sums, change, second, *images = call(
         step_kernel, (shape(8, BLK), FIELD, FIELD) + PARTS, [SMEM] + [VMEM] * 5,
         SCRATCH, operator_flops, operator_bytes,
     )(slots, partial, lift, schur, image, projected)
     dots = ((0, 0), (0, None), (1, None), (0, 2))
-    second_image, terms = combine(dots, places, swaps, lengths, split, images, second, projected, image)
+    second_image, terms = combine(dots, places, layout, split, images, second, projected, image)
 
     partial = coarse_solve(core, table, terms)
-    multipliers, norm = call(
-        last_kernel, (shape(2, SLOTS * BLK, BLK), shape(places, 8, BLK)), [SMEM] + [VMEM] * 8,
-        [SCRATCH[0], SCRATCH[2]],
-    )(slots, partial, lift, sums, start, projected, change, second, second_image)
-    norm = jnp.sum(lax.all_to_all(norm, "p", 0, 0, tiled=True), axis=0)
+    norm, scale = call(
+        last_kernel, (shape(places, NORM_ROWS, BLK), shape(8, BLK)), [VMEM] * 6, [SCRATCH[0]]
+    )(partial, lift, sums, change, second, second_image)
+    norm = lax.all_to_all(norm, "p", 0, 0, tiled=True)
+    multipliers, mark = call(
+        multipliers_kernel, (shape(2, SLOTS * BLK, BLK), MARK), [SMEM] + [VMEM] * 5, [SCRATCH[0], SCRATCH[2]], room=60
+    )(slots, scale, started, lift, projected, second)
+    norm = call(total_kernel, shape(NORM_ROWS, BLK), [VMEM, ANY])(norm, mark)
     norm = norm + lax.ppermute(norm, "core", [(0, 1), (1, 0)])
-    norm = lax.all_to_all(jnp.broadcast_to(norm[None], (4, 8, BLK)), "x", 0, 0, tiled=True)
+    norm = lax.all_to_all(jnp.broadcast_to(norm[None], (4, NORM_ROWS, BLK)), "x", 0, 0, tiled=True)
     return multipliers, jnp.sqrt(jnp.sum(norm[:, 0], axis=0) / sums[4])
 
 

time: 209 us -> 206 us (0.986)
  blocking collectives: 94.7 us -> 81.4 us
  starting transfers between devices: 52.2 us -> 56.9 us
  Pallas kernels: 23.4 us -> 27.3 us
  waiting for transfers between devices: 26.9 us -> 30.4 us
    all_to_all x2 -> x1, blocking collectives: 19.7 us -> 6.43 us  [body(): lax.all_to_all(jnp.broadcast_to(norm[None], (4, NORM_ROWS, BLK)), 'x', 0,...]
    all_to_all x0 -> x1, waiting for transfers between devices: none -> 4.71 us  [body(): norm = lax.all_to_all(norm, 'p', 0, 0, tiled=True)]
    all_to_all x0 -> x1, starting transfers between devices: none -> 4.23 us  [body(): norm = lax.all_to_all(norm, 'p', 0, 0, tiled=True)]
    pallas_call x5 -> x7, Pallas kernels: 7.97 us -> 10.5 us  [the longest x1 3.9 us: body(): call(multipliers_kernel, (shape(2, SLOTS * BLK, BLK), MARK), [SMEM] + [VM...]
    unnamed x26 -> x28, local copies, waits for them, and re-layouts: 9.14 us -> 7.32 us
  transfers between devices with their start and end apart: 22 -> 23, of which waited for: 17 -> 18; matrix products, arithmetic and copies ran while one was open for 0% -> 0% of each run, Pallas kernels for 0% -> 2%
where the time goes in v3:
time: 206 us
  blocking collectives  81.4 us (40%)
  starting transfers between devices  56.9 us (28%)
  waiting for transfers between devices  30.4 us (15%)
  Pallas kernels  27.3 us (13%)
  local copies, waits for them, and re-layouts  7.33 us (4%)
    all_to_all x3, blocking collectives, coarse_solve(): gathered = lax.all_to_all(terms, 'p', 0, 0, tiled=True)  42.4 us
    all_to_all x4, blocking collectives, collect(): return lax.all_to_all(both, 'x', 0, 0, tiled=True)  32.6 us
    ppermute x16, starting transfers between devices, moved(): lax.ppermute(value, axis, [(i, (i + step) % count) for i in range(count)])  21.5 us
    ppermute x16, waiting for transfers between devices, moved(): lax.ppermute(value, axis, [(i, (i + step) % count) for i in range(count)])  20.6 us
    ppermute x4, starting transfers between devices, collect(): both = mine + lax.ppermute(other, 'core', [(0, 1), (1, 0)])  15.7 us
    all_to_all x1, starting transfers between devices, unpack(): payload = lax.all_to_all(payload, 'p', 0, 0, tiled=True)  12.2 us
    unnamed x28, local copies, waits for them, and re-layouts  7.32 us
    all_to_all x1, blocking collectives, body(): lax.all_to_all(jnp.broadcast_to(norm[None], (4, NORM_ROWS, BLK)), 'x', 0,...  6.43 us
  transfers between devices with their start and end apart: 23, of which 18 were waited for; matrix products, arithmetic and copies ran while one was open for 0% of the time, Pallas kernels for 2%

profile of v3, /device:TPU:1, one launch (start us, length us, event | category | flops | bytes accessed | tf_op | source)
XLA Modules:
  0.0 205.5 jit_solution(9918712956935839031)
XLA Ops:
  0.6 3.2 %shard_map.95 = (bf16[2,32,1536]{2,1,0:T(8,128)(2,1)}, f32[32,32,128]{2,1,0:T(8,128)}, f32[2,12,8,128]{3,2,1,0:T(8,128)}, f32[2,2,8,128]{3,2,1,0:T(8,128)}, f32[...) custom-call(s32[2,12]{1,0:T(2,128)} %slot_ref.9, f32[6,2,1536]{2,1,0:T(2,128)} %bitcast.12, ...), custom_call_target="tpu_custom_call" | custom-call | tf_op jit(solution)/shard_map/pallas_call | solution.py:83
  3.9 12.2 %all-to-all-start = ((f32[32,32,128]{2,1,0:T(8,128)}), f32[32,32,128]{2,1,0:T(8,128)S(1)}, u32[]{:S(2)}, u32[]{:S(2)}) async-start(f32[32,32,128]{2,1,0:T(8,128)} %get-tuple-element.48), calls=%async_computation | async-start | bytes 1048576 | tf_op jit(solution)/shard_map/all_to_all | solution.py:163
  16.0 1.3 collective-permute-start
  17.3 1.5 collective-permute-start.1
  18.8 2.9 %collective-permute-start.2 = (f32[2,2,8,128]{3,2,1,0:T(8,128)}, f32[2,2,8,128]{3,2,1,0:T(8,128)S(1)}, u32[]{:S(2)}, u32[]{:S(2)}) collective-permute-start(f32[2,2,8,128]{3,2,1,0:T(8,128)} %get-tuple-element.52), channel_id=1, source_target_pairs={{0,4},{4,8},{8,12},{12,16},{16,20},{20,24},{24,28},{28,32},{32,36}... | collective-permute-start | bytes 49160 | tf_op jit(solution)/shard_map/ppermute | solution.py:347
  22.5 2.3 %collective-permute-done.2.rest_2_ = f32[2,2,8,128]{3,2,1,0:T(8,128)S(1)} collective-permute-done((f32[2,2,8,128]{3,2,1,0:T(8,128)}, f32[2,2,8,128]{3,2,1,0:T(8,128)S(1)}, u32[]{:S(2)}, u32[]{:S(2)}) %collective-permute-start.2) | collective-permute-done | bytes 16416 | tf_op jit(solution)/shard_map/ppermute | solution.py:347
  24.8 5.3 %collective-permute-done.3.rest_3_ = f32[2,2,8,128]{3,2,1,0:T(8,128)S(1)} collective-permute-done((f32[2,2,8,128]{3,2,1,0:T(8,128)}, f32[2,2,8,128]{3,2,1,0:T(8,128)S(1)}, u32[]{:S(2)}, u32[]{:S(2)}) %collective-permute-start.3) | collective-permute-done | bytes 16416 | tf_op jit(solution)/shard_map/ppermute | solution.py:347
  31.3 1.2 shard_map.96
  32.5 4.3 %collective-permute-start.4 = (f32[4,64,128]{2,1,0:T(8,128)S(1)}, f32[4,64,128]{2,1,0:T(8,128)S(1)}, u32[]{:S(2)}, u32[]{:S(2)}) collective-permute-start(f32[4,64,128]{2,1,0:T(8,128)S(1)} %get-tuple-element.57), channel_id=1, source_target_pairs={{0,4},{4,0},{1,5},{5,1},{2,6},{6,2},{3,7},{7,3},{8,12},{12,8},{9,1... | collective-permute-start | bytes 393224 | tf_op jit(solution)/shard_map/ppermute | solution.py:173
  36.8 1.0 collective-permute-done.4
  37.8 8.6 %all_to_all.50.partial_ref = f32[4,64,128]{2,1,0:T(8,128)S(1)} all-to-all(f32[4,64,128]{2,1,0:T(8,128)S(1)} %add.15), channel_id=1, replica_groups=mesh['p'=32,'core'=2,'x'=4] {'x'}, dimensions={0} | all-to-all | bytes 262144 | tf_op jit(solution)/shard_map/all_to_all | solution.py:174
  46.4 3.7 %copy-done = bf16[2,1536,1536]{2,1,0:T(8,128)(2,1)S(1)} copy-done((bf16[2,1536,1536]{2,1,0:T(8,128)(2,1)S(1)}, bf16[2,1536,1536]{2,1,0:T(8,128)(2,1)}, u32[]{:S(2)}) %copy-start) | copy-done | bytes 9437208
  50.2 1.4 copy-done.5
  51.6 3.7 %shard_map.97 = (f32[2,4,128,128]{3,2,1,0:T(8,128)S(1)}, f32[2,2,128,128]{3,2,1,0:T(8,128)S(1)}, f32[2,2,128,128]{3,2,1,0:T(8,128)S(1)}, f32[2,2,128,128]{3,2,1,0:T(8,128)S(1)}, f32[2,2,128,128]{3,2,1,0:T(8,128)S(1)}) custom-call(s32[2,12]{1,0:T(2,128)S(1)} %copy-done.8, f32[4,64,128]{2,1,0:T(8,128)S(1)} %all_to_all.50.partial_ref, ...), custom_call_target="tpu_custom_call" | custom-call | flops 1207959552 | bytes 9437184 | tf_op jit(solution)/shard_map/pallas_call | solution.py:375
  56.9 2.4 %collective-permute-start.8 = (f32[2,2,128,128]{3,2,1,0:T(8,128)S(1)}, f32[2,2,128,128]{3,2,1,0:T(8,128)S(1)}, u32[]{:S(2)}, u32[]{:S(2)}) collective-permute-start(f32[2,2,128,128]{3,2,1,0:T(8,128)S(1)} %get-tuple-element.62.rest_3_), channel_id=1, source_target_pairs={{0,252},{4,0},{8,4},{12,8},{16,12},{20,16},{24,20},{28,24},{32,28}... | collective-permute-start | bytes 786440 | tf_op jit(solution)/shard_map/ppermute | solution.py:347
  59.2 1.5 collective-permute-start.7
  61.4 1.8 collective-permute-done.5.rest_5_
  63.2 1.8 collective-permute-done.8.rest_8_
  65.0 1.4 shard_map.98
  66.5 14.0 %all_to_all.51.terms_ref = f32[32,16,128]{2,1,0:T(8,128)S(1)} all-to-all(f32[32,16,128]{2,1,0:T(8,128)S(1)} %get-tuple-element.64), channel_id=1, replica_groups=mesh['p'=32,'core'=2,'x'=4] {'p'}, dimensions={0} | all-to-all | bytes 524288 | tf_op jit(solution)/shard_map/all_to_all | solution.py:178
  81.1 3.9 %collective-permute-start.9 = (f32[4,64,128]{2,1,0:T(8,128)S(1)}, f32[4,64,128]{2,1,0:T(8,128)S(1)}, u32[]{:S(2)}, u32[]{:S(2)}) collective-permute-start(f32[4,64,128]{2,1,0:T(8,128)S(1)} %get-tuple-element.66), channel_id=1, source_target_pairs={{0,4},{4,0},{1,5},{5,1},{2,6},{6,2},{3,7},{7,3},{8,12},{12,8},{9,1... | collective-permute-start | bytes 393224 | tf_op jit(solution)/shard_map/ppermute | solution.py:173
  85.0 1.0 collective-permute-done.9
  86.0 8.0 %all_to_all.52.partial_ref = f32[4,64,128]{2,1,0:T(8,128)S(1)} all-to-all(f32[4,64,128]{2,1,0:T(8,128)S(1)} %add.16), channel_id=1, replica_groups=mesh['p'=32,'core'=2,'x'=4] {'x'}, dimensions={0} | all-to-all | bytes 262144 | tf_op jit(solution)/shard_map/all_to_all | solution.py:174
  94.0 3.6 %shard_map.100 = (f32[2,12,128,128]{3,2,1,0:T(8,128)S(1)}, f32[2,4,128,128]{3,2,1,0:T(8,128)S(1)}, f32[2,2,128,128]{3,2,1,0:T(8,128)S(1)}, f32[2,2,128,128]{3,2,...) custom-call(s32[2,12]{1,0:T(2,128)S(1)} %copy-done.8, ...), custom_call_target="tpu_custom_call" | custom-call | flops 1207959552 | bytes 9437184 | tf_op jit(solution)/shard_map/pallas_call | solution.py:382
  99.2 2.3 %collective-permute-start.13 = (f32[2,2,128,128]{3,2,1,0:T(8,128)S(1)}, f32[2,2,128,128]{3,2,1,0:T(8,128)S(1)}, u32[]{:S(2)}, u32[]{:S(2)}) collective-permute-start(f32[2,2,128,128]{3,2,1,0:T(8,128)S(1)} %get-tuple-element.71.rest_3_), channel_id=1, source_target_pairs={{0,252},{4,0},{8,4},{12,8},{16,12},{20,16},{24,20},{28,24},{32,28}... | collective-permute-start | bytes 786440 | tf_op jit(solution)/shard_map/ppermute | solution.py:347
  101.6 1.3 collective-permute-start.12
  103.8 1.8 collective-permute-done.10.rest_5_
  105.6 1.7 collective-permute-done.13.rest_8_
  107.2 1.6 shard_map.101
  108.9 14.2 %all_to_all.53.terms_ref = f32[32,16,128]{2,1,0:T(8,128)S(1)} all-to-all(f32[32,16,128]{2,1,0:T(8,128)S(1)} %get-tuple-element.74), channel_id=1, replica_groups=mesh['p'=32,'core'=2,'x'=4] {'p'}, dimensions={0} | all-to-all | bytes 524288 | tf_op jit(solution)/shard_map/all_to_all | solution.py:178
  123.6 3.7 %collective-permute-start.14 = (f32[4,64,128]{2,1,0:T(8,128)S(1)}, f32[4,64,128]{2,1,0:T(8,128)S(1)}, u32[]{:S(2)}, u32[]{:S(2)}) collective-permute-start(f32[4,64,128]{2,1,0:T(8,128)S(1)} %get-tuple-element.76), channel_id=1, source_target_pairs={{0,4},{4,0},{1,5},{5,1},{2,6},{6,2},{3,7},{7,3},{8,12},{12,8},{9,1... | collective-permute-start | bytes 393224 | tf_op jit(solution)/shard_map/ppermute | solution.py:173
  128.3 8.0 %all_to_all.54.partial_ref = f32[4,64,128]{2,1,0:T(8,128)S(1)} all-to-all(f32[4,64,128]{2,1,0:T(8,128)S(1)} %add.17), channel_id=1, replica_groups=mesh['p'=32,'core'=2,'x'=4] {'x'}, dimensions={0} | all-to-all | bytes 262144 | tf_op jit(solution)/shard_map/all_to_all | solution.py:174
  136.3 3.7 %shard_map.103 = (f32[8,128]{1,0:T(8,128)S(1)}, f32[2,12,128,128]{3,2,1,0:T(8,128)S(1)}, f32[2,12,128,128]{3,2,1,0:T(8,128)S(1)}, f32[2,4,128,128]{3,2,1,0:T(8,1...) custom-call(s32[2,12]{1,0:T(2,128)S(1)} %copy-done.8, ...), custom_call_target="tpu_custom_call" | custom-call | flops 1207959552 | bytes 9437184 | tf_op jit(solution)/shard_map/pallas_call | solution.py:388
  141.6 2.4 %collective-permute-start.18 = (f32[2,2,128,128]{3,2,1,0:T(8,128)S(1)}, f32[2,2,128,128]{3,2,1,0:T(8,128)S(1)}, u32[]{:S(2)}, u32[]{:S(2)}) collective-permute-start(f32[2,2,128,128]{3,2,1,0:T(8,128)S(1)} %get-tuple-element.81.rest_3_), channel_id=1, source_target_pairs={{0,252},{4,0},{8,4},{12,8},{16,12},{20,16},{24,20},{28,24},{32,28}... | collective-permute-start | bytes 786440 | tf_op jit(solution)/shard_map/ppermute | solution.py:347
  143.9 1.4 collective-permute-start.17
  146.1 1.8 collective-permute-done.15.rest_5_
  147.9 1.7 collective-permute-done.18.rest_8_
  149.6 1.9 shard_map.104
  151.6 14.2 %all_to_all.55.terms_ref = f32[32,16,128]{2,1,0:T(8,128)S(1)} all-to-all(f32[32,16,128]{2,1,0:T(8,128)S(1)} %get-tuple-element.84), channel_id=1, replica_groups=mesh['p'=32,'core'=2,'x'=4] {'p'}, dimensions={0} | all-to-all | bytes 524288 | tf_op jit(solution)/shard_map/all_to_all | solution.py:178
  166.3 3.7 %collective-permute-start.19 = (f32[4,64,128]{2,1,0:T(8,128)S(1)}, f32[4,64,128]{2,1,0:T(8,128)S(1)}, u32[]{:S(2)}, u32[]{:S(2)}) collective-permute-start(f32[4,64,128]{2,1,0:T(8,128)S(1)} %get-tuple-element.86), channel_id=1, source_target_pairs={{0,4},{4,0},{1,5},{5,1},{2,6},{6,2},{3,7},{7,3},{8,12},{12,8},{9,1... | collective-permute-start | bytes 393224 | tf_op jit(solution)/shard_map/ppermute | solution.py:173
  170.0 1.0 collective-permute-done.19
  171.0 8.0 %all_to_all.56.partial_ref = f32[4,64,128]{2,1,0:T(8,128)S(1)} all-to-all(f32[4,64,128]{2,1,0:T(8,128)S(1)} %add.18), channel_id=1, replica_groups=mesh['p'=32,'core'=2,'x'=4] {'x'}, dimensions={0} | all-to-all | bytes 262144 | tf_op jit(solution)/shard_map/all_to_all | solution.py:174
  179.0 1.3 shard_map.106
  180.8 4.2 %all-to-all-start.8 = ((f32[32,1,128]{2,1,0:T(1,128)}), f32[32,1,128]{2,1,0:T(1,128)S(1)}, u32[]{:S(2)}, u32[]{:S(2)}) async-start(f32[32,1,128]{2,1,0:T(1,128)} %get-tuple-element.92), calls=%async_computation.8 | async-start | bytes 32768 | tf_op jit(solution)/shard_map/all_to_all | solution.py:399
  185.1 3.9 %shard_map.107 = (f32[2,1536,128]{2,1,0:T(8,128)}, f32[8,128]{1,0:T(8,128)}) custom-call(s32[2,12]{1,0:T(2,128)} %slot_ref.9, f32[8,128]{1,0:T(8,128)} %copy-done.10, f32[4,64,128]{2,1,0:T(8,128)} %copy-done.6, bf16[2,6,256,96]{3,2,1,0:T(8,128)(2,1)} %copy-done.2, f32[2,12,128,128]{3,2,1,0:T(8,128)} %copy-done.1, f32[2,12,128,128]{3,2,1,0:T(8,128)} %copy-done.3), custom_call_target="tpu_custom_call" | custom-call | tf_op jit(solution)/shard_map/pallas_call | solution.py:400
  189.0 4.7 %all-to-all-done.8.norm_ref = f32[32,1,128]{2,1,0:T(1,128)S(1)} async-done(((f32[32,1,128]{2,1,0:T(1,128)}), f32[32,1,128]{2,1,0:T(1,128)S(1)}, u32[]{:S(2)}, u32[]{:S(2)}) %all-to-all-start.8) | async-done | bytes 16416 | tf_op jit(solution)/shard_map/all_to_all | solution.py:399
  194.4 3.3 %collective-permute-start.20 = (f32[1,128]{1,0:T(1,128)S(1)}, f32[1,128]{1,0:T(1,128)S(1)}, u32[]{:S(2)}, u32[]{:S(2)}) collective-permute-start(f32[1,128]{1,0:T(1,128)S(1)} %shard_map.108), channel_id=1, source_target_pairs={{0,4},{4,0},{1,5},{5,1},{2,6},{6,2},{3,7},{7,3},{8,12},{12,8},{9,1... | collective-permute-start | bytes 1544 | tf_op jit(solution)/shard_map/ppermute | solution.py:404
  198.6 6.4 %all_to_all.57 = f32[4,1,128]{2,1,0:T(1,128)S(1)} all-to-all(f32[4,1,128]{2,1,0:T(1,128)S(1)} %broadcast_in_dim.13), channel_id=1, replica_groups=mesh['p'=32,'core'=2,'x'=4] {'x'}, dimensions={0} | all-to-all | bytes 4096 | tf_op jit(solution)/shard_map/all_to_all | solution.py:405
  (58 shorter events, 14.3 us)
Async XLA Ops:
  0.6 45.8 %copy-start.8 = (s32[2,12]{1,0:T(2,128)S(1)}, s32[2,12]{1,0:T(2,128)}, u32[]{:S(2)}) copy-start(s32[2,12]{1,0:T(2,128)} %slot_ref.9) | copy-start | bytes 292
  3.9 76.7 %slice-start = ((s8[9437184]{0:T(1024)(128)(4,1)}), s8[1048576]{0:T(1024)(128)(4,1)S(1)}, s32[]{:S(2)}) async-start(s8[9437184]{0:T(1024)(128)(4,1)} %bitcast.10), calls=%async_computation.10 | async-start | bytes 2097152
  3.9 26.5 %all-to-all-start = ((f32[32,32,128]{2,1,0:T(8,128)}), f32[32,32,128]{2,1,0:T(8,128)S(1)}, u32[]{:S(2)}, u32[]{:S(2)}) async-start(f32[32,32,128]{2,1,0:T(8,128)} %get-tuple-element.48), calls=%async_computation | async-start | bytes 1048576 | tf_op jit(solution)/shard_map/all_to_all | solution.py:163
  16.0 6.4 %collective-permute-start = (f32[2,2,8,128]{3,2,1,0:T(8,128)}, f32[2,2,8,128]{3,2,1,0:T(8,128)S(1)}, u32[]{:S(2)}, u32[]{:S(2)}) collective-permute-start(f32[2,2,8,128]{3,2,1,0:T(8,128)} %get-tuple-element.50), channel_id=1, source_target_pairs={{0,1},{1,2},{2,3},{3,0},{4,5},{5,6},{6,7},{7,4},{8,9},{9,10},{10,1... | collective-permute-start | bytes 49160 | tf_op jit(solution)/shard_map/ppermute | solution.py:347
  17.3 5.2 %collective-permute-start.1 = (f32[2,2,8,128]{3,2,1,0:T(8,128)}, f32[2,2,8,128]{3,2,1,0:T(8,128)S(1)}, u32[]{:S(2)}, u32[]{:S(2)}) collective-permute-start(f32[2,2,8,128]{3,2,1,0:T(8,128)} %get-tuple-element.51), channel_id=1, source_target_pairs={{0,3},{1,0},{2,1},{3,2},{4,7},{5,4},{6,5},{7,6},{8,11},{9,8},{10,9... | collective-permute-start | bytes 49160 | tf_op jit(solution)/shard_map/ppermute | solution.py:347
  18.8 6.0 %collective-permute-start.2 = (f32[2,2,8,128]{3,2,1,0:T(8,128)}, f32[2,2,8,128]{3,2,1,0:T(8,128)S(1)}, u32[]{:S(2)}, u32[]{:S(2)}) collective-permute-start(f32[2,2,8,128]{3,2,1,0:T(8,128)} %get-tuple-element.52), channel_id=1, source_target_pairs={{0,4},{4,8},{8,12},{12,16},{16,20},{20,24},{24,28},{28,32},{32,36}... | collective-permute-start | bytes 49160 | tf_op jit(solution)/shard_map/ppermute | solution.py:347
  21.7 8.4 %collective-permute-start.3 = (f32[2,2,8,128]{3,2,1,0:T(8,128)}, f32[2,2,8,128]{3,2,1,0:T(8,128)S(1)}, u32[]{:S(2)}, u32[]{:S(2)}) collective-permute-start(f32[2,2,8,128]{3,2,1,0:T(8,128)} %get-tuple-element.53), channel_id=1, source_target_pairs={{0,252},{4,0},{8,4},{12,8},{16,12},{20,16},{24,20},{28,24},{32,28}... | collective-permute-start | bytes 49160 | tf_op jit(solution)/shard_map/ppermute | solution.py:347
  30.4 0.9 copy-start.7
  32.5 146.5 %copy-start.2 = (bf16[2,6,256,96]{3,2,1,0:T(8,128)(2,1)}, bf16[2,6,256,96]{3,2,1,0:T(8,128)(2,1)S(1)}, u32[]{:S(2)}) copy-start(bf16[2,6,256,96]{3,2,1,0:T(8,128)(2,1)S(1)} %get-tuple-element.58.lift_ref) | copy-start | bytes 1769476
  32.5 5.2 %collective-permute-start.4 = (f32[4,64,128]{2,1,0:T(8,128)S(1)}, f32[4,64,128]{2,1,0:T(8,128)S(1)}, u32[]{:S(2)}, u32[]{:S(2)}) collective-permute-start(f32[4,64,128]{2,1,0:T(8,128)S(1)} %get-tuple-element.57), channel_id=1, source_target_pairs={{0,4},{4,0},{1,5},{5,1},{2,6},{6,2},{3,7},{7,3},{8,12},{12,8},{9,1... | collective-permute-start | bytes 393224 | tf_op jit(solution)/shard_map/ppermute | solution.py:173
  46.4 8.9 %copy-start.6 = (f32[4,64,128]{2,1,0:T(8,128)}, f32[4,64,128]{2,1,0:T(8,128)S(1)}, u32[]{:S(2)}) copy-start(f32[4,64,128]{2,1,0:T(8,128)S(1)} %all_to_all.50.partial_ref) | copy-start | bytes 393220
  46.4 3.7 %copy-start = (bf16[2,1536,1536]{2,1,0:T(8,128)(2,1)S(1)}, bf16[2,1536,1536]{2,1,0:T(8,128)(2,1)}, u32[]{:S(2)}) copy-start(bf16[2,1536,1536]{2,1,0:T(8,128)(2,1)} %schur_ref.5) | copy-start | bytes 28311556
  50.2 1.4 copy-start.5
  51.6 13.5 %copy-start.4 = (bf16[2,32,1536]{2,1,0:T(8,128)(2,1)S(1)}, bf16[2,32,1536]{2,1,0:T(8,128)(2,1)}, u32[]{:S(2)}) copy-start(bf16[2,32,1536]{2,1,0:T(8,128)(2,1)} %get-tuple-element.55.split_ref) | copy-start | bytes 589828
  51.6 29.0 %slice-start.1 = ((s8[9437184]{0:T(1024)(128)(4,1)}), s8[4194304]{0:T(1024)(128)(4,1)S(1)}, s32[]{:S(2)}) async-start(s8[9437184]{0:T(1024)(128)(4,1)} %bitcast.10), calls=%async_computation.11 | async-start | bytes 8388608
  51.6 29.0 %slice-start.2 = ((s8[9437184]{0:T(1024)(128)(4,1)}), s8[4194304]{0:T(1024)(128)(4,1)S(1)}, s32[]{:S(2)}) async-start(s8[9437184]{0:T(1024)(128)(4,1)} %bitcast.10), calls=%async_computation.12 | async-start | bytes 8388608
  55.3 6.1 %collective-permute-start.6 = (f32[2,2,128,128]{3,2,1,0:T(8,128)S(1)}, f32[2,2,128,128]{3,2,1,0:T(8,128)S(1)}, u32[]{:S(2)}, u32[]{:S(2)}) collective-permute-start(f32[2,2,128,128]{3,2,1,0:T(8,128)S(1)} %get-tuple-element.60.rest_1_), channel_id=1, source_target_pairs={{0,3},{1,0},{2,1},{3,2},{4,7},{5,4},{6,5},{7,6},{8,11},{9,8},{10,9... | collective-permute-start | bytes 786440 | tf_op jit(solution)/shard_map/ppermute | solution.py:347
  56.3 6.9 %collective-permute-start.5 = (f32[2,2,128,128]{3,2,1,0:T(8,128)S(1)}, f32[2,2,128,128]{3,2,1,0:T(8,128)S(1)}, u32[]{:S(2)}, u32[]{:S(2)}) collective-permute-start(f32[2,2,128,128]{3,2,1,0:T(8,128)S(1)} %get-tuple-element.61.rest_2_), channel_id=1, source_target_pairs={{0,1},{1,2},{2,3},{3,0},{4,5},{5,6},{6,7},{7,4},{8,9},{9,10},{10,1... | collective-permute-start | bytes 786440 | tf_op jit(solution)/shard_map/ppermute | solution.py:347
  56.9 8.2 %collective-permute-start.8 = (f32[2,2,128,128]{3,2,1,0:T(8,128)S(1)}, f32[2,2,128,128]{3,2,1,0:T(8,128)S(1)}, u32[]{:S(2)}, u32[]{:S(2)}) collective-permute-start(f32[2,2,128,128]{3,2,1,0:T(8,128)S(1)} %get-tuple-element.62.rest_3_), channel_id=1, source_target_pairs={{0,252},{4,0},{8,4},{12,8},{16,12},{20,16},{24,20},{28,24},{32,28}... | collective-permute-start | bytes 786440 | tf_op jit(solution)/shard_map/ppermute | solution.py:347
  59.2 5.8 %collective-permute-start.7 = (f32[2,2,128,128]{3,2,1,0:T(8,128)S(1)}, f32[2,2,128,128]{3,2,1,0:T(8,128)S(1)}, u32[]{:S(2)}, u32[]{:S(2)}) collective-permute-start(f32[2,2,128,128]{3,2,1,0:T(8,128)S(1)} %get-tuple-element.63.rest_4_), channel_id=1, source_target_pairs={{0,4},{4,8},{8,12},{12,16},{16,20},{20,24},{24,28},{28,32},{32,36}... | collective-permute-start | bytes 786440 | tf_op jit(solution)/shard_map/ppermute | solution.py:347
  81.1 4.9 %collective-permute-start.9 = (f32[4,64,128]{2,1,0:T(8,128)S(1)}, f32[4,64,128]{2,1,0:T(8,128)S(1)}, u32[]{:S(2)}, u32[]{:S(2)}) collective-permute-start(f32[4,64,128]{2,1,0:T(8,128)S(1)} %get-tuple-element.66), channel_id=1, source_target_pairs={{0,4},{4,0},{1,5},{5,1},{2,6},{6,2},{3,7},{7,3},{8,12},{12,8},{9,1... | collective-permute-start | bytes 393224 | tf_op jit(solution)/shard_map/ppermute | solution.py:173
  97.7 52.0 %copy-start.1 = (f32[2,12,128,128]{3,2,1,0:T(8,128)}, f32[2,12,128,128]{3,2,1,0:T(8,128)S(1)}, u32[]{:S(2)}) copy-start(f32[2,12,128,128]{3,2,1,0:T(8,128)S(1)} %get-tuple-element.73.rest_9_.projected_ref.rest_10_.first_ref) | copy-start | bytes 4718596
  97.7 6.1 %collective-permute-start.11 = (f32[2,2,128,128]{3,2,1,0:T(8,128)S(1)}, f32[2,2,128,128]{3,2,1,0:T(8,128)S(1)}, u32[]{:S(2)}, u32[]{:S(2)}) collective-permute-start(f32[2,2,128,128]{3,2,1,0:T(8,128)S(1)} %get-tuple-element.69.rest_1_), channel_id=1, source_target_pairs={{0,3},{1,0},{2,1},{3,2},{4,7},{5,4},{6,5},{7,6},{8,11},{9,8},{10,9... | collective-permute-start | bytes 786440 | tf_op jit(solution)/shard_map/ppermute | solution.py:347
  98.6 6.9 %collective-permute-start.10 = (f32[2,2,128,128]{3,2,1,0:T(8,128)S(1)}, f32[2,2,128,128]{3,2,1,0:T(8,128)S(1)}, u32[]{:S(2)}, u32[]{:S(2)}) collective-permute-start(f32[2,2,128,128]{3,2,1,0:T(8,128)S(1)} %get-tuple-element.70.rest_2_), channel_id=1, source_target_pairs={{0,1},{1,2},{2,3},{3,0},{4,5},{5,6},{6,7},{7,4},{8,9},{9,10},{10,1... | collective-permute-start | bytes 786440 | tf_op jit(solution)/shard_map/ppermute | solution.py:347
  99.2 8.0 %collective-permute-start.13 = (f32[2,2,128,128]{3,2,1,0:T(8,128)S(1)}, f32[2,2,128,128]{3,2,1,0:T(8,128)S(1)}, u32[]{:S(2)}, u32[]{:S(2)}) collective-permute-start(f32[2,2,128,128]{3,2,1,0:T(8,128)S(1)} %get-tuple-element.71.rest_3_), channel_id=1, source_target_pairs={{0,252},{4,0},{8,4},{12,8},{16,12},{20,16},{24,20},{28,24},{32,28}... | collective-permute-start | bytes 786440 | tf_op jit(solution)/shard_map/ppermute | solution.py:347
  101.6 5.7 %collective-permute-start.12 = (f32[2,2,128,128]{3,2,1,0:T(8,128)S(1)}, f32[2,2,128,128]{3,2,1,0:T(8,128)S(1)}, u32[]{:S(2)}, u32[]{:S(2)}) collective-permute-start(f32[2,2,128,128]{3,2,1,0:T(8,128)S(1)} %get-tuple-element.72.rest_4_), channel_id=1, source_target_pairs={{0,4},{4,8},{8,12},{12,16},{16,20},{20,24},{24,28},{28,32},{32,36}... | collective-permute-start | bytes 786440 | tf_op jit(solution)/shard_map/ppermute | solution.py:347
  123.6 4.7 %collective-permute-start.14 = (f32[4,64,128]{2,1,0:T(8,128)S(1)}, f32[4,64,128]{2,1,0:T(8,128)S(1)}, u32[]{:S(2)}, u32[]{:S(2)}) collective-permute-start(f32[4,64,128]{2,1,0:T(8,128)S(1)} %get-tuple-element.76), channel_id=1, source_target_pairs={{0,4},{4,0},{1,5},{5,1},{2,6},{6,2},{3,7},{7,3},{8,12},{12,8},{9,1... | collective-permute-start | bytes 393224 | tf_op jit(solution)/shard_map/ppermute | solution.py:173
  140.0 39.0 %copy-start.3 = (f32[2,12,128,128]{3,2,1,0:T(8,128)}, f32[2,12,128,128]{3,2,1,0:T(8,128)S(1)}, u32[]{:S(2)}) copy-start(f32[2,12,128,128]{3,2,1,0:T(8,128)S(1)} %get-tuple-element.83.rest_9_.second_ref) | copy-start | bytes 4718596
  140.0 6.1 %collective-permute-start.16 = (f32[2,2,128,128]{3,2,1,0:T(8,128)S(1)}, f32[2,2,128,128]{3,2,1,0:T(8,128)S(1)}, u32[]{:S(2)}, u32[]{:S(2)}) collective-permute-start(f32[2,2,128,128]{3,2,1,0:T(8,128)S(1)} %get-tuple-element.79.rest_1_), channel_id=1, source_target_pairs={{0,3},{1,0},{2,1},{3,2},{4,7},{5,4},{6,5},{7,6},{8,11},{9,8},{10,9... | collective-permute-start | bytes 786440 | tf_op jit(solution)/shard_map/ppermute | solution.py:347
  141.0 6.9 %collective-permute-start.15 = (f32[2,2,128,128]{3,2,1,0:T(8,128)S(1)}, f32[2,2,128,128]{3,2,1,0:T(8,128)S(1)}, u32[]{:S(2)}, u32[]{:S(2)}) collective-permute-start(f32[2,2,128,128]{3,2,1,0:T(8,128)S(1)} %get-tuple-element.80.rest_2_), channel_id=1, source_target_pairs={{0,1},{1,2},{2,3},{3,0},{4,5},{5,6},{6,7},{7,4},{8,9},{9,10},{10,1... | collective-permute-start | bytes 786440 | tf_op jit(solution)/shard_map/ppermute | solution.py:347
  141.6 8.0 %collective-permute-start.18 = (f32[2,2,128,128]{3,2,1,0:T(8,128)S(1)}, f32[2,2,128,128]{3,2,1,0:T(8,128)S(1)}, u32[]{:S(2)}, u32[]{:S(2)}) collective-permute-start(f32[2,2,128,128]{3,2,1,0:T(8,128)S(1)} %get-tuple-element.81.rest_3_), channel_id=1, source_target_pairs={{0,252},{4,0},{8,4},{12,8},{16,12},{20,16},{24,20},{28,24},{32,28}... | collective-permute-start | bytes 786440 | tf_op jit(solution)/shard_map/ppermute | solution.py:347
  143.9 5.7 %collective-permute-start.17 = (f32[2,2,128,128]{3,2,1,0:T(8,128)S(1)}, f32[2,2,128,128]{3,2,1,0:T(8,128)S(1)}, u32[]{:S(2)}, u32[]{:S(2)}) collective-permute-start(f32[2,2,128,128]{3,2,1,0:T(8,128)S(1)} %get-tuple-element.82.rest_4_), channel_id=1, source_target_pairs={{0,4},{4,8},{8,12},{12,16},{16,20},{20,24},{24,28},{28,32},{32,36}... | collective-permute-start | bytes 786440 | tf_op jit(solution)/shard_map/ppermute | solution.py:347
  166.3 4.7 %collective-permute-start.19 = (f32[4,64,128]{2,1,0:T(8,128)S(1)}, f32[4,64,128]{2,1,0:T(8,128)S(1)}, u32[]{:S(2)}, u32[]{:S(2)}) collective-permute-start(f32[4,64,128]{2,1,0:T(8,128)S(1)} %get-tuple-element.86), channel_id=1, source_target_pairs={{0,4},{4,0},{1,5},{5,1},{2,6},{6,2},{3,7},{7,3},{8,12},{12,8},{9,1... | collective-permute-start | bytes 393224 | tf_op jit(solution)/shard_map/ppermute | solution.py:173
  180.2 0.6 copy-start.10
  180.8 12.9 %all-to-all-start.8 = ((f32[32,1,128]{2,1,0:T(1,128)}), f32[32,1,128]{2,1,0:T(1,128)S(1)}, u32[]{:S(2)}, u32[]{:S(2)}) async-start(f32[32,1,128]{2,1,0:T(1,128)} %get-tuple-element.92), calls=%async_computation.8 | async-start | bytes 32768 | tf_op jit(solution)/shard_map/all_to_all | solution.py:399
  193.7 0.7 copy-start.9
  194.4 4.2 %collective-permute-start.20 = (f32[1,128]{1,0:T(1,128)S(1)}, f32[1,128]{1,0:T(1,128)S(1)}, u32[]{:S(2)}, u32[]{:S(2)}) collective-permute-start(f32[1,128]{1,0:T(1,128)S(1)} %shard_map.108), channel_id=1, source_target_pairs={{0,4},{4,0},{1,5},{5,1},{2,6},{6,2},{3,7},{7,3},{8,12},{12,8},{9,1... | collective-permute-start | bytes 1544 | tf_op jit(solution)/shard_map/ppermute | solution.py:404
